TPU v7x, 32 devices: a whole 2x2x4 slice. The times are simulated.
32 devices in a mesh: seq: 16 (over z, y, core), head: 2 (over x).
Axes of the slice: x: 2, y: 2, z: 4, core: 2. Of those that a mesh axis runs over, the one named last changes fastest.
Arguments:
- prefix_embed: bfloat16 [256, 1024], replicated, may hold values from -6 to 6
- w_hidden: bfloat16 [1024, 8192], P(None, 'seq'), may hold values from -0.1875 to 0.1875
- b_hidden: float32 [8192], P('seq'), may hold values from -4 to 4
- w_out: bfloat16 [8192, 2, 1024], P('seq', None, 'head'), may hold values from -0.0625 to 0.0625
- queries: bfloat16 [2048, 8192], P('seq', 'head'), may hold values from -6 to 6
- keys: bfloat16 [2048, 1024], P('seq', 'head'), may hold values from -6 to 6
- values: bfloat16 [2048, 1024], P('seq', 'head'), may hold values from -6 to 6
- out_grad: bfloat16 [2048, 8192], P('seq', 'head'), may hold values from -6 to 6
Outputs:
- query_grad: bfloat16 [2048, 8192], P('seq', 'head')
- grad_w_out: float32 [8192, 2, 1024], P('seq', None, 'head')
- grad_w_hidden: float32 [1024, 8192], P(None, 'seq')
- grad_b_hidden: float32 [8192], P('seq')
- grad_prefix: float32 [256, 1024], replicated
All inputs are finite; a program needn't handle non-finite values.
Results may differ from a plain program's by a relative error of at most 0.008.
Values may be sent and summed in bfloat16 or wider, within the bound.
A program may use at most 64 MiB of HBM per device.

v0:
```python
import math

import jax
import jax.numpy as jnp
from jax import lax
from jax.sharding import PartitionSpec as P

QH = 64
KVH = 8
HD = 128


def shifted(value, axis, steps):
    count = lax.axis_size(axis)
    first, last = (max(0, -steps), min(count, count - steps))
    return lax.ppermute(value, axis, [(source, source + steps) for source in range(first, last)])


def key_sweep(running, key_part, value_part, offset, bounds, update):
    seq_start, last_pos = bounds
    key_count = key_part.shape[0]
    block_len = math.gcd(key_count, 512)
    heads_here = key_part.shape[1] // HD

    def advance(turn, held):
        first_key = offset + turn * block_len
        key_block = lax.dynamic_slice_in_dim(key_part, turn * block_len, block_len, 0).reshape(
            block_len, heads_here, HD
        )
        value_block = lax.dynamic_slice_in_dim(value_part, turn * block_len, block_len, 0).reshape(
            block_len, heads_here, HD
        )
        useful = (first_key <= last_pos) & (first_key + block_len - 1 >= seq_start)
        return lax.cond(
            useful,
            lambda kept: update(kept, key_block, value_block, first_key),
            lambda kept: kept,
            held,
        )

    return lax.fori_loop(0, key_count // block_len, advance, running)


def on_device(prefix_embed, w_hidden, b_hidden, w_out, queries, keys, values, out_grad):
    scaling = 1.0 / math.sqrt(HD)
    group = QH // KVH
    hidden_pre = jnp.dot(prefix_embed, w_hidden, preferred_element_type=jnp.float32) + b_hidden
    tangent = jnp.tanh(hidden_pre)
    hidden = tangent.astype(jnp.bfloat16)
    partial_kv = jnp.einsum("ph,hck->pck", hidden, w_out, preferred_element_type=jnp.float32)
    prefix_kv = lax.psum(partial_kv, "seq").astype(jnp.bfloat16)
    tok_count = queries.shape[0]
    span = lax.axis_size("seq")
    seq_length = tok_count * span
    heads_here = keys.shape[1] // HD
    prefix_len = prefix_kv.shape[0]
    prefix_keys = prefix_kv[:, 0].reshape(prefix_len, heads_here, HD)
    prefix_values = prefix_kv[:, 1].reshape(prefix_len, heads_here, HD)

    def by_head(rows):
        return (
            rows.reshape(tok_count, heads_here, group, HD)
            .transpose(1, 0, 2, 3)
            .reshape(heads_here, tok_count * group, HD)
        )

    query_rows = by_head(queries)
    grad_rows = by_head(out_grad)
    my_start = lax.axis_index("seq") * tok_count
    last_pos = my_start + tok_count - 1
    seq_start = my_start // seq_length * seq_length
    bounds = (seq_start, last_pos)
    query_pos = my_start + jnp.arange(tok_count * group, dtype=jnp.int32) // group
    local_pair = jnp.stack([keys, values], 0)

    def block_scores(key_block, value_block, first_key):
        logits = (
            jnp.einsum("grd,ngd->grn", query_rows, key_block, preferred_element_type=jnp.float32)
            * scaling
        )
        dot_grads = jnp.einsum(
            "grd,ngd->grn", grad_rows, value_block, preferred_element_type=jnp.float32
        )
        key_pos = first_key + jnp.arange(key_block.shape[0], dtype=jnp.int32)
        seen = (key_pos[None, None, :] <= query_pos[None, :, None]) & (
            key_pos[None, None, :] >= seq_start
        )
        logits = jnp.where(seen, logits, -1e30)
        return (logits, dot_grads)

    def forward_update(running, key_block, value_block, first_key):
        run_max, run_sum, run_dot = running
        logits, dot_grads = block_scores(key_block, value_block, first_key)
        new_max = jnp.maximum(run_max, jnp.max(logits, axis=-1))
        rescale = jnp.exp(run_max - new_max)
        weights = jnp.exp(logits - new_max[..., None])
        return (
            new_max,
            run_sum * rescale + jnp.sum(weights, axis=-1),
            run_dot * rescale + jnp.sum(weights * dot_grads, axis=-1),
        )

    prefix_logits = (
        jnp.einsum("grd,ngd->grn", query_rows, prefix_keys, preferred_element_type=jnp.float32)
        * scaling
    )
    prefix_dots = jnp.einsum(
        "grd,ngd->grn", grad_rows, prefix_values, preferred_element_type=jnp.float32
    )
    start_max = jnp.max(prefix_logits, axis=-1)
    start_weights = jnp.exp(prefix_logits - start_max[..., None])
    start_state = (
        start_max,
        jnp.sum(start_weights, axis=-1),
        jnp.sum(start_weights * prefix_dots, axis=-1),
    )
    start_state = key_sweep(start_state, keys, values, my_start, bounds, forward_update)
    held_empty = jnp.zeros((span,) + local_pair.shape, local_pair.dtype)
    held_empty = held_empty.at[span - 1].set(local_pair)

    def collect_turn(turn, carry):
        held, piece = carry
        moved = shifted(piece, "seq", 1)
        held = lax.dynamic_update_index_in_dim(held, moved, span - 2 - turn, 0)
        return (held, moved)

    held, unused = lax.fori_loop(0, span - 1, collect_turn, (held_empty, local_pair))
    earlier = held[: span - 1]
    key_all = earlier[:, 0].reshape((span - 1) * tok_count, keys.shape[1])
    value_all = earlier[:, 1].reshape((span - 1) * tok_count, keys.shape[1])
    earliest = my_start - (span - 1) * tok_count
    final_state = key_sweep(start_state, key_all, value_all, earliest, bounds, forward_update)
    run_max, run_sum, run_dot = final_state
    log_total = run_max + jnp.log(run_sum)
    delta_row = run_dot / run_sum

    def backward_update(total, key_block, value_block, first_key):
        logits, dot_grads = block_scores(key_block, value_block, first_key)
        probs = jnp.exp(logits - log_total[..., None])
        score_grad = (probs * (dot_grads - delta_row[..., None])).astype(jnp.bfloat16)
        return total + jnp.einsum(
            "grn,ngd->grd", score_grad, key_block, preferred_element_type=jnp.float32
        )

    prefix_probs = jnp.exp(prefix_logits - log_total[..., None])
    prefix_score_grad = (prefix_probs * (prefix_dots - delta_row[..., None])).astype(jnp.bfloat16)
    start_total = jnp.einsum(
        "grn,ngd->grd", prefix_score_grad, prefix_keys, preferred_element_type=jnp.float32
    )
    start_total = key_sweep(start_total, keys, values, my_start, bounds, backward_update)
    total = key_sweep(start_total, key_all, value_all, earliest, bounds, backward_update)
    query_grad = (total * scaling).reshape(heads_here, tok_count, group, HD).transpose(1, 0, 2, 3)
    query_grad = query_grad.reshape(tok_count, heads_here * group * HD).astype(jnp.bfloat16)
    key_grad = (
        jnp.einsum(
            "grn,grd->ngd", prefix_score_grad, query_rows, preferred_element_type=jnp.float32
        )
        * scaling
    )
    value_grad = jnp.einsum(
        "grn,grd->ngd",
        prefix_probs.astype(jnp.bfloat16),
        grad_rows,
        preferred_element_type=jnp.float32,
    )
    both_grads = jnp.stack(
        [
            key_grad.reshape(prefix_len, heads_here * HD),
            value_grad.reshape(prefix_len, heads_here * HD),
        ],
        1,
    )
    prefix_grads = lax.psum(both_grads, "seq").astype(jnp.bfloat16)
    grad_w_out = jnp.einsum("ph,pck->hck", hidden, prefix_grads, preferred_element_type=jnp.float32)
    hidden_part = jnp.einsum("pck,hck->ph", prefix_grads, w_out, preferred_element_type=jnp.float32)
    hidden_grad = lax.psum(hidden_part, "head")
    pre_grad = hidden_grad * (1.0 - tangent * tangent)
    pre_rounded = pre_grad.astype(jnp.bfloat16)
    grad_w_hidden = lax.dot_general(
        prefix_embed, pre_rounded, (((0,), (0,)), ((), ())), preferred_element_type=jnp.float32
    )
    grad_b_hidden = jnp.sum(pre_grad, axis=0)
    embed_part = lax.dot_general(
        pre_rounded, w_hidden, (((1,), (1,)), ((), ())), preferred_element_type=jnp.float32
    )
    grad_prefix = lax.psum(embed_part, "seq")
    return (query_grad, grad_w_out, grad_w_hidden, grad_b_hidden, grad_prefix)


def solution(mesh):
    placed = (
        P(),
        P(None, "seq"),
        P("seq"),
        P("seq", None, "head"),
        P("seq", "head"),
        P("seq", "head"),
        P("seq", "head"),
        P("seq", "head"),
    )
    return jax.shard_map(
        on_device,
        mesh=mesh,
        in_specs=placed,
        out_specs=(P("seq", "head"), P("seq", None, "head"), P(None, "seq"), P("seq"), P()),
        check_vma=False,
    )
```

profile of v0, /device:TPU:0, one launch (start us, length us, event | category | flops | bytes accessed | tf_op | source)
XLA Modules:
  0.0 638.3 jit_solution(4828886484015446554)
XLA Ops:
  8.8 1.7 copy.135
  10.5 1.8 fusion.40
  13.6 74.8 %all-reduce.9 = bf16[256,2,512]{2,0,1:T(8,128)(2,1)S(1)} all-reduce(f32[256,2,512]{2,0,1:T(8,128)S(1)} %fusion.43), channel_id=1, replica_groups=mesh['seq'=16,'head'=2] {'seq'}, use_global_device_ids=true, to_apply=%region_0.0 | all-reduce | flops 262144 | bytes 1572864 | tf_op jit(solution)/shard_map/psum | solution.py:51
  90.3 1.7 reshape_squeeze.13
  92.1 1.2 copy.176
  93.3 1.2 copy.177
  94.5 2.4 scatter.4
  96.9 116.7 %while.73 = (s32[]{:T(128)}, bf16[16,2,128,512]{3,2,1,0:T(8,128)(2,1)}, bf16[2,128,512]{2,1,0:T(8,128)(2,1)S(1)}, s32[]{:T(128)}, s32[]{:T(128)}, /*index=5*/s32[]{:T(128)}, s32[]{:T(128)}) while((s32[]{:T(128)}, bf16[16,2,128,512]{3,2,1,0:T(8,128)(2,1)}, bf16[2,128,512]{2,1,0:T(8,128)(2,1)S(1)}, s32[]{:T(128)}, s32[]{:T(128)}, ...), condition=%wide.region_10.11_spmd, body=%wide.region_9.10_spmd.sunk | while | flops 6 | bytes 2097327 | solution.py:127
  96.9 1.3 collective-permute-start
  98.2 1.1 collective-permute-done
  100.1 2.3 collective-permute-start
  102.4 1.1 collective-permute-done
  104.2 5.6 collective-permute-start
  109.8 1.1 collective-permute-done
  111.6 6.5 %collective-permute-start = (bf16[2,128,512]{2,1,0:T(8,128)(2,1)S(1)}, bf16[2,128,512]{2,1,0:T(8,128)(2,1)S(1)}, u32[]{:S(2)}, u32[]{:S(2)}) collective-permute-start(bf16[2,128,512]{2,1,0:T(8,128)(2,1)S(1)} %get-tuple-element.1915), channel_id=1, source_target_pairs={{0,2},{2,4},{4,6},{6,8},{8,10},{10,12},{12,14},{14,16},{16,18},{18... | collective-permute-start | bytes 786440 | tf_op jit(solution)/shard_map/while/body/eval_jaxpr/ppermute | solution.py:16
  118.2 1.1 collective-permute-done
  120.1 6.5 %collective-permute-start = (bf16[2,128,512]{2,1,0:T(8,128)(2,1)S(1)}, bf16[2,128,512]{2,1,0:T(8,128)(2,1)S(1)}, u32[]{:S(2)}, u32[]{:S(2)}) collective-permute-start(bf16[2,128,512]{2,1,0:T(8,128)(2,1)S(1)} %get-tuple-element.1915), channel_id=1, source_target_pairs={{0,2},{2,4},{4,6},{6,8},{8,10},{10,12},{12,14},{14,16},{16,18},{18... | collective-permute-start | bytes 786440 | tf_op jit(solution)/shard_map/while/body/eval_jaxpr/ppermute | solution.py:16
  126.6 1.1 collective-permute-done
  128.5 6.5 %collective-permute-start = (bf16[2,128,512]{2,1,0:T(8,128)(2,1)S(1)}, bf16[2,128,512]{2,1,0:T(8,128)(2,1)S(1)}, u32[]{:S(2)}, u32[]{:S(2)}) collective-permute-start(bf16[2,128,512]{2,1,0:T(8,128)(2,1)S(1)} %get-tuple-element.1915), channel_id=1, source_target_pairs={{0,2},{2,4},{4,6},{6,8},{8,10},{10,12},{12,14},{14,16},{16,18},{18... | collective-permute-start | bytes 786440 | tf_op jit(solution)/shard_map/while/body/eval_jaxpr/ppermute | solution.py:16
  135.1 1.1 collective-permute-done
  136.9 6.5 %collective-permute-start = (bf16[2,128,512]{2,1,0:T(8,128)(2,1)S(1)}, bf16[2,128,512]{2,1,0:T(8,128)(2,1)S(1)}, u32[]{:S(2)}, u32[]{:S(2)}) collective-permute-start(bf16[2,128,512]{2,1,0:T(8,128)(2,1)S(1)} %get-tuple-element.1915), channel_id=1, source_target_pairs={{0,2},{2,4},{4,6},{6,8},{8,10},{10,12},{12,14},{14,16},{16,18},{18... | collective-permute-start | bytes 786440 | tf_op jit(solution)/shard_map/while/body/eval_jaxpr/ppermute | solution.py:16
  143.5 1.1 collective-permute-done
  145.4 6.5 %collective-permute-start = (bf16[2,128,512]{2,1,0:T(8,128)(2,1)S(1)}, bf16[2,128,512]{2,1,0:T(8,128)(2,1)S(1)}, u32[]{:S(2)}, u32[]{:S(2)}) collective-permute-start(bf16[2,128,512]{2,1,0:T(8,128)(2,1)S(1)} %get-tuple-element.1915), channel_id=1, source_target_pairs={{0,2},{2,4},{4,6},{6,8},{8,10},{10,12},{12,14},{14,16},{16,18},{18... | collective-permute-start | bytes 786440 | tf_op jit(solution)/shard_map/while/body/eval_jaxpr/ppermute | solution.py:16
  151.9 1.1 collective-permute-done
  153.8 6.5 %collective-permute-start = (bf16[2,128,512]{2,1,0:T(8,128)(2,1)S(1)}, bf16[2,128,512]{2,1,0:T(8,128)(2,1)S(1)}, u32[]{:S(2)}, u32[]{:S(2)}) collective-permute-start(bf16[2,128,512]{2,1,0:T(8,128)(2,1)S(1)} %get-tuple-element.1915), channel_id=1, source_target_pairs={{0,2},{2,4},{4,6},{6,8},{8,10},{10,12},{12,14},{14,16},{16,18},{18... | collective-permute-start | bytes 786440 | tf_op jit(solution)/shard_map/while/body/eval_jaxpr/ppermute | solution.py:16
  160.3 1.1 collective-permute-done
  162.2 6.5 %collective-permute-start = (bf16[2,128,512]{2,1,0:T(8,128)(2,1)S(1)}, bf16[2,128,512]{2,1,0:T(8,128)(2,1)S(1)}, u32[]{:S(2)}, u32[]{:S(2)}) collective-permute-start(bf16[2,128,512]{2,1,0:T(8,128)(2,1)S(1)} %get-tuple-element.1915), channel_id=1, source_target_pairs={{0,2},{2,4},{4,6},{6,8},{8,10},{10,12},{12,14},{14,16},{16,18},{18... | collective-permute-start | bytes 786440 | tf_op jit(solution)/shard_map/while/body/eval_jaxpr/ppermute | solution.py:16
  168.8 1.1 collective-permute-done
  170.6 6.5 %collective-permute-start = (bf16[2,128,512]{2,1,0:T(8,128)(2,1)S(1)}, bf16[2,128,512]{2,1,0:T(8,128)(2,1)S(1)}, u32[]{:S(2)}, u32[]{:S(2)}) collective-permute-start(bf16[2,128,512]{2,1,0:T(8,128)(2,1)S(1)} %get-tuple-element.1915), channel_id=1, source_target_pairs={{0,2},{2,4},{4,6},{6,8},{8,10},{10,12},{12,14},{14,16},{16,18},{18... | collective-permute-start | bytes 786440 | tf_op jit(solution)/shard_map/while/body/eval_jaxpr/ppermute | solution.py:16
  177.2 1.1 collective-permute-done
  179.0 6.5 %collective-permute-start = (bf16[2,128,512]{2,1,0:T(8,128)(2,1)S(1)}, bf16[2,128,512]{2,1,0:T(8,128)(2,1)S(1)}, u32[]{:S(2)}, u32[]{:S(2)}) collective-permute-start(bf16[2,128,512]{2,1,0:T(8,128)(2,1)S(1)} %get-tuple-element.1915), channel_id=1, source_target_pairs={{0,2},{2,4},{4,6},{6,8},{8,10},{10,12},{12,14},{14,16},{16,18},{18... | collective-permute-start | bytes 786440 | tf_op jit(solution)/shard_map/while/body/eval_jaxpr/ppermute | solution.py:16
  187.5 6.5 %collective-permute-start = (bf16[2,128,512]{2,1,0:T(8,128)(2,1)S(1)}, bf16[2,128,512]{2,1,0:T(8,128)(2,1)S(1)}, u32[]{:S(2)}, u32[]{:S(2)}) collective-permute-start(bf16[2,128,512]{2,1,0:T(8,128)(2,1)S(1)} %get-tuple-element.1915), channel_id=1, source_target_pairs={{0,2},{2,4},{4,6},{6,8},{8,10},{10,12},{12,14},{14,16},{16,18},{18... | collective-permute-start | bytes 786440 | tf_op jit(solution)/shard_map/while/body/eval_jaxpr/ppermute | solution.py:16
  195.9 6.5 %collective-permute-start = (bf16[2,128,512]{2,1,0:T(8,128)(2,1)S(1)}, bf16[2,128,512]{2,1,0:T(8,128)(2,1)S(1)}, u32[]{:S(2)}, u32[]{:S(2)}) collective-permute-start(bf16[2,128,512]{2,1,0:T(8,128)(2,1)S(1)} %get-tuple-element.1915), channel_id=1, source_target_pairs={{0,2},{2,4},{4,6},{6,8},{8,10},{10,12},{12,14},{14,16},{16,18},{18... | collective-permute-start | bytes 786440 | tf_op jit(solution)/shard_map/while/body/eval_jaxpr/ppermute | solution.py:16
  204.3 7.4 %collective-permute-start = (bf16[2,128,512]{2,1,0:T(8,128)(2,1)S(1)}, bf16[2,128,512]{2,1,0:T(8,128)(2,1)S(1)}, u32[]{:S(2)}, u32[]{:S(2)}) collective-permute-start(bf16[2,128,512]{2,1,0:T(8,128)(2,1)S(1)} %get-tuple-element.1915), channel_id=1, source_target_pairs={{0,2},{2,4},{4,6},{6,8},{8,10},{10,12},{12,14},{14,16},{16,18},{18... | collective-permute-start | bytes 786440 | tf_op jit(solution)/shard_map/while/body/eval_jaxpr/ppermute | solution.py:16
  213.6 3.8 fusion.67
  217.3 2.3 copy.141
  219.6 4.1 copy.140
  223.8 2.7 copy_bitcast_fusion.1
  227.2 2.0 copy-done.2
  229.2 3.7 fusion.29
  232.9 5.6 conditional.4
  234.5 2.0 multiply_reduce_fusion
  238.5 17.8 %while.74 = (s32[]{:T(128)}, f32[4,1024]{1,0:T(4,128)S(1)}, f32[4,1024]{1,0:T(4,128)}, f32[4,1024]{1,0:T(4,128)}, s32[]{:T(128)}, /*index=5*/s32[]{:T(128)}, s32...) while((s32[]{:T(128)}, f32[4,1024]{1,0:T(4,128)S(1)}, ...), condition=%wide.region_17.18_spmd.clone, body=%wide.region_11.0_spmd.clone.sunk | while | flops 272913792 | bytes 10028845 | solution.py:41
  256.3 1.4 log_add_fusion
  257.7 4.1 fusion.36
  261.8 3.4 fusion.31
  265.3 1.6 convolution_multiply_fusion
  266.9 2.0 copy.153
  269.0 2.0 copy.154
  271.0 1.3 pad_maximum_fusion
  272.3 157.0 %all-reduce.10 = bf16[256,2,512]{2,0,1:T(8,128)(2,1)} all-reduce(f32[256,2,512]{2,0,1:T(8,128)S(1)} %pad_maximum_fusion), channel_id=1, replica_groups=mesh['seq'=16,'head'=2] {'seq'}, use_global_device_ids=true, to_apply=%region_24.25 | all-reduce | flops 262144 | bytes 1572864 | tf_op jit(solution)/shard_map/psum | solution.py:173
  429.3 2.3 convolution_bitcast_fusion.1
  431.7 3.8 fusion.52
  435.6 4.9 conditional.5
  436.5 3.9 convolution_add_fusion
  441.5 1.8 fusion.41
  443.6 1.4 copy.206
  445.0 12.7 %all-reduce.6.cloned.1.call-done = f32[256,512]{1,0:T(8,128)} async-done(((f32[256,512]{1,0:T(8,128)}), f32[256,512]{1,0:T(8,128)}) %all-reduce.6.cloned.1.call-update) | async-done | bytes 524304 | tf_op jit(solution)/shard_map/psum | solution.py:176
  457.7 1.7 fusion.56
  459.4 1.4 fusion.71
  461.3 2.9 copy.157
  464.7 1.8 copy.158
  466.6 162.6 %all-reduce.8.cloned.1.call-done = f32[256,1024]{1,0:T(8,128)} async-done(((f32[256,1024]{1,0:T(8,128)}), f32[256,1024]{1,0:T(8,128)}) %all-reduce.8.cloned.1.call-update) | async-done | bytes 1048592 | tf_op jit(solution)/shard_map/psum | solution.py:186
  629.2 2.3 copy.259
  (200 shorter events, 45.9 us)
Async XLA Ops:
  7.2 6.0 copy-start
  7.2 450.5 %all-reduce.6.cloned.1.call-start = ((), (), s32[]{:S(2)}) async-start(), calls=%async_computation | async-start | bytes 1048576 | tf_op jit(solution)/shard_map/psum | solution.py:176
  12.3 0.8 copy-start.8
  88.4 3.7 copy-start.14
  89.2 4.0 copy-start.15
  92.1 2.4 copy-start.26
  92.1 2.4 copy-start.27
  96.9 2.4 collective-permute-start
  100.1 3.4 collective-permute-start
  104.2 6.7 %collective-permute-start = (bf16[2,128,512]{2,1,0:T(8,128)(2,1)S(1)}, bf16[2,128,512]{2,1,0:T(8,128)(2,1)S(1)}, u32[]{:S(2)}, u32[]{:S(2)}) collective-permute-start(bf16[2,128,512]{2,1,0:T(8,128)(2,1)S(1)} %get-tuple-element.1915), channel_id=1, source_target_pairs={{0,2},{2,4},{4,6},{6,8},{8,10},{10,12},{12,14},{14,16},{16,18},{18... | collective-permute-start | bytes 786440 | tf_op jit(solution)/shard_map/while/body/eval_jaxpr/ppermute | solution.py:16
  111.6 7.7 %collective-permute-start = (bf16[2,128,512]{2,1,0:T(8,128)(2,1)S(1)}, bf16[2,128,512]{2,1,0:T(8,128)(2,1)S(1)}, u32[]{:S(2)}, u32[]{:S(2)}) collective-permute-start(bf16[2,128,512]{2,1,0:T(8,128)(2,1)S(1)} %get-tuple-element.1915), channel_id=1, source_target_pairs={{0,2},{2,4},{4,6},{6,8},{8,10},{10,12},{12,14},{14,16},{16,18},{18... | collective-permute-start | bytes 786440 | tf_op jit(solution)/shard_map/while/body/eval_jaxpr/ppermute | solution.py:16
  120.1 7.7 %collective-permute-start = (bf16[2,128,512]{2,1,0:T(8,128)(2,1)S(1)}, bf16[2,128,512]{2,1,0:T(8,128)(2,1)S(1)}, u32[]{:S(2)}, u32[]{:S(2)}) collective-permute-start(bf16[2,128,512]{2,1,0:T(8,128)(2,1)S(1)} %get-tuple-element.1915), channel_id=1, source_target_pairs={{0,2},{2,4},{4,6},{6,8},{8,10},{10,12},{12,14},{14,16},{16,18},{18... | collective-permute-start | bytes 786440 | tf_op jit(solution)/shard_map/while/body/eval_jaxpr/ppermute | solution.py:16
  128.5 7.7 %collective-permute-start = (bf16[2,128,512]{2,1,0:T(8,128)(2,1)S(1)}, bf16[2,128,512]{2,1,0:T(8,128)(2,1)S(1)}, u32[]{:S(2)}, u32[]{:S(2)}) collective-permute-start(bf16[2,128,512]{2,1,0:T(8,128)(2,1)S(1)} %get-tuple-element.1915), channel_id=1, source_target_pairs={{0,2},{2,4},{4,6},{6,8},{8,10},{10,12},{12,14},{14,16},{16,18},{18... | collective-permute-start | bytes 786440 | tf_op jit(solution)/shard_map/while/body/eval_jaxpr/ppermute | solution.py:16
  136.9 7.7 %collective-permute-start = (bf16[2,128,512]{2,1,0:T(8,128)(2,1)S(1)}, bf16[2,128,512]{2,1,0:T(8,128)(2,1)S(1)}, u32[]{:S(2)}, u32[]{:S(2)}) collective-permute-start(bf16[2,128,512]{2,1,0:T(8,128)(2,1)S(1)} %get-tuple-element.1915), channel_id=1, source_target_pairs={{0,2},{2,4},{4,6},{6,8},{8,10},{10,12},{12,14},{14,16},{16,18},{18... | collective-permute-start | bytes 786440 | tf_op jit(solution)/shard_map/while/body/eval_jaxpr/ppermute | solution.py:16
  145.4 7.7 %collective-permute-start = (bf16[2,128,512]{2,1,0:T(8,128)(2,1)S(1)}, bf16[2,128,512]{2,1,0:T(8,128)(2,1)S(1)}, u32[]{:S(2)}, u32[]{:S(2)}) collective-permute-start(bf16[2,128,512]{2,1,0:T(8,128)(2,1)S(1)} %get-tuple-element.1915), channel_id=1, source_target_pairs={{0,2},{2,4},{4,6},{6,8},{8,10},{10,12},{12,14},{14,16},{16,18},{18... | collective-permute-start | bytes 786440 | tf_op jit(solution)/shard_map/while/body/eval_jaxpr/ppermute | solution.py:16
  153.8 7.7 %collective-permute-start = (bf16[2,128,512]{2,1,0:T(8,128)(2,1)S(1)}, bf16[2,128,512]{2,1,0:T(8,128)(2,1)S(1)}, u32[]{:S(2)}, u32[]{:S(2)}) collective-permute-start(bf16[2,128,512]{2,1,0:T(8,128)(2,1)S(1)} %get-tuple-element.1915), channel_id=1, source_target_pairs={{0,2},{2,4},{4,6},{6,8},{8,10},{10,12},{12,14},{14,16},{16,18},{18... | collective-permute-start | bytes 786440 | tf_op jit(solution)/shard_map/while/body/eval_jaxpr/ppermute | solution.py:16
  162.2 7.7 %collective-permute-start = (bf16[2,128,512]{2,1,0:T(8,128)(2,1)S(1)}, bf16[2,128,512]{2,1,0:T(8,128)(2,1)S(1)}, u32[]{:S(2)}, u32[]{:S(2)}) collective-permute-start(bf16[2,128,512]{2,1,0:T(8,128)(2,1)S(1)} %get-tuple-element.1915), channel_id=1, source_target_pairs={{0,2},{2,4},{4,6},{6,8},{8,10},{10,12},{12,14},{14,16},{16,18},{18... | collective-permute-start | bytes 786440 | tf_op jit(solution)/shard_map/while/body/eval_jaxpr/ppermute | solution.py:16
  170.6 7.7 %collective-permute-start = (bf16[2,128,512]{2,1,0:T(8,128)(2,1)S(1)}, bf16[2,128,512]{2,1,0:T(8,128)(2,1)S(1)}, u32[]{:S(2)}, u32[]{:S(2)}) collective-permute-start(bf16[2,128,512]{2,1,0:T(8,128)(2,1)S(1)} %get-tuple-element.1915), channel_id=1, source_target_pairs={{0,2},{2,4},{4,6},{6,8},{8,10},{10,12},{12,14},{14,16},{16,18},{18... | collective-permute-start | bytes 786440 | tf_op jit(solution)/shard_map/while/body/eval_jaxpr/ppermute | solution.py:16
  179.0 7.7 %collective-permute-start = (bf16[2,128,512]{2,1,0:T(8,128)(2,1)S(1)}, bf16[2,128,512]{2,1,0:T(8,128)(2,1)S(1)}, u32[]{:S(2)}, u32[]{:S(2)}) collective-permute-start(bf16[2,128,512]{2,1,0:T(8,128)(2,1)S(1)} %get-tuple-element.1915), channel_id=1, source_target_pairs={{0,2},{2,4},{4,6},{6,8},{8,10},{10,12},{12,14},{14,16},{16,18},{18... | collective-permute-start | bytes 786440 | tf_op jit(solution)/shard_map/while/body/eval_jaxpr/ppermute | solution.py:16
  187.5 7.7 %collective-permute-start = (bf16[2,128,512]{2,1,0:T(8,128)(2,1)S(1)}, bf16[2,128,512]{2,1,0:T(8,128)(2,1)S(1)}, u32[]{:S(2)}, u32[]{:S(2)}) collective-permute-start(bf16[2,128,512]{2,1,0:T(8,128)(2,1)S(1)} %get-tuple-element.1915), channel_id=1, source_target_pairs={{0,2},{2,4},{4,6},{6,8},{8,10},{10,12},{12,14},{14,16},{16,18},{18... | collective-permute-start | bytes 786440 | tf_op jit(solution)/shard_map/while/body/eval_jaxpr/ppermute | solution.py:16
  195.9 7.7 %collective-permute-start = (bf16[2,128,512]{2,1,0:T(8,128)(2,1)S(1)}, bf16[2,128,512]{2,1,0:T(8,128)(2,1)S(1)}, u32[]{:S(2)}, u32[]{:S(2)}) collective-permute-start(bf16[2,128,512]{2,1,0:T(8,128)(2,1)S(1)} %get-tuple-element.1915), channel_id=1, source_target_pairs={{0,2},{2,4},{4,6},{6,8},{8,10},{10,12},{12,14},{14,16},{16,18},{18... | collective-permute-start | bytes 786440 | tf_op jit(solution)/shard_map/while/body/eval_jaxpr/ppermute | solution.py:16
  204.3 8.5 %collective-permute-start = (bf16[2,128,512]{2,1,0:T(8,128)(2,1)S(1)}, bf16[2,128,512]{2,1,0:T(8,128)(2,1)S(1)}, u32[]{:S(2)}, u32[]{:S(2)}) collective-permute-start(bf16[2,128,512]{2,1,0:T(8,128)(2,1)S(1)} %get-tuple-element.1915), channel_id=1, source_target_pairs={{0,2},{2,4},{4,6},{6,8},{8,10},{10,12},{12,14},{14,16},{16,18},{18... | collective-permute-start | bytes 786440 | tf_op jit(solution)/shard_map/while/body/eval_jaxpr/ppermute | solution.py:16
  219.6 4.1 copy-start.4
  223.8 2.7 copy-start.5
  226.5 2.7 copy-start.13
  227.2 2.0 copy-start.2
  232.9 1.5 copy-start.24
  236.5 0.7 copy-start.16
  236.5 0.7 copy-start.20
  237.3 0.6 copy-start.17
  237.9 0.6 copy-start.21
  257.7 4.1 copy-start.3
  261.8 3.5 copy-start.6
  265.3 1.7 copy-start.7
  431.6 3.9 copy-start.28
  431.7 197.5 %all-reduce.8.cloned.1.call-start = ((), (), s32[]{:S(2)}) async-start(), calls=%async_computation.1 | async-start | bytes 2097152 | tf_op jit(solution)/shard_map/psum | solution.py:186
  435.6 0.9 copy-start.25
  443.4 14.3 %copy-start.9 = (f32[256,512]{1,0:T(8,128)S(1)}, f32[256,512]{1,0:T(8,128)}, u32[]{:S(2)}) copy-start(f32[256,512]{1,0:T(8,128)} %copy-done.8) | copy-start | bytes 1572868
  443.6 15.8 %copy-start.10 = (bf16[1024,512]{1,0:T(8,128)(2,1)S(1)}, bf16[1024,512]{1,0:T(8,128)(2,1)}, u32[]{:S(2)}) copy-start(bf16[1024,512]{1,0:T(8,128)(2,1)} %param.25) | copy-start | bytes 3145732
  445.0 15.9 %copy-start.12 = (bf16[256,2,512]{2,0,1:T(8,128)(2,1)S(1)}, bf16[256,2,512]{2,0,1:T(8,128)(2,1)}, u32[]{:S(2)}) copy-start(bf16[256,2,512]{2,0,1:T(8,128)(2,1)} %all-reduce.10) | copy-start | bytes 1572868
  461.3 3.0 copy-start.11
  464.7 166.7 %copy-start.1 = (bf16[512,2,512]{2,1,0:T(2,128)(2,1)S(1)}, bf16[512,2,512]{2,1,0:T(2,128)(2,1)}, u32[]{:S(2)}) copy-start(bf16[512,2,512]{2,1,0:T(2,128)(2,1)} %param.27) | copy-start | bytes 3145732
Sparse Core Ops, SparseCore 0:
  431.8 25.8 all-reduce.5
  462.1 167.0 all-reduce.7
where the time goes:
time: 641 us; the launch traced here: 638 us
  blocking collectives  232 us (36%)
  waiting for transfers between devices  192 us (30%)
  starting transfers between devices  88.6 us (14%)
  local copies, waits for them, and re-layouts  61.3 us (10%)
  matrix products  28 us (4%)
  other arithmetic  20.8 us (3%)
  between operations  14.2 us (2%)
    psum x1, waiting for transfers between devices, on_device(): grad_prefix = lax.psum(embed_part, 'seq')  163 us
    psum x1, blocking collectives, on_device(): prefix_grads = lax.psum(both_grads, 'seq').astype(jnp.bfloat16)  157 us
    ppermute x15, starting transfers between devices, shifted(): lax.ppermute(value, axis, [(source, source + steps) for source in range(f...  88.5 us
    psum x1, blocking collectives, on_device(): prefix_kv = lax.psum(partial_kv, 'seq').astype(jnp.bfloat16)  74.8 us
    unnamed x48, local copies, waits for them, and re-layouts  22.9 us
    ppermute x15, waiting for transfers between devices, shifted(): lax.ppermute(value, axis, [(source, source + steps) for source in range(f...  16.8 us
  transfers between devices with their start and end apart: 17, of which 17 were waited for; matrix products, arithmetic and copies ran while one was open for 3% of the time, Pallas kernels for 0%

commit v1 on v0

v1 whole, which is shorter than its diff:
```python
import functools
import math

import jax
import jax.numpy as jnp
from jax import lax
from jax.experimental import pallas as pl
from jax.experimental.pallas import tpu as pltpu
from jax.sharding import PartitionSpec as P

QH = 64
KVH = 8
HD = 128
HEADS_PER_TILE = 4


def dot(a, b, dims):
    return lax.dot_general(a, b, (dims, ((), ())), preferred_element_type=jnp.float32)


NT = ((1,), (1,))
NN = ((1,), (0,))
TN = ((0,), (0,))


def fold_lanes(block, op):
    parts = [block[:, i : i + HD] for i in range(0, block.shape[1], HD)]
    return functools.reduce(op, parts)


def attention_kernel(
    pos_ref, q_ref, do_ref, k_ref, v_ref, pk_ref, pv_ref,
    dq_ref, kg_ref, vg_ref,
    q_s, do_s, s_s, d_s, ps_s, pd_s, m_s, l_s, dl_s, acc_s,
):
    tok = q_ref.shape[0]
    heads = q_ref.shape[1] // HD
    block = s_s.shape[2]
    scaling = 1.0 / math.sqrt(HD)
    to_exp2 = scaling * math.log2(math.e)
    my_start = pos_ref[0] * tok
    full = my_start // block

    for h in range(heads):
        q_s[h * tok : (h + 1) * tok, :] = q_ref[:, h * HD : (h + 1) * HD]
        do_s[h * tok : (h + 1) * tok, :] = do_ref[:, h * HD : (h + 1) * HD]

    s = dot(q_s[...], pk_ref[...], NT)
    ps_s[...] = s
    m_s[...] = fold_lanes(s, jnp.maximum)

    def logits(i):
        return dot(q_s[...], k_ref[pl.ds(pl.multiple_of(i * block, block), block), :], NT)

    def first(i, carry):
        s = logits(i)
        s_s[i] = s
        m_s[...] = jnp.maximum(m_s[...], fold_lanes(s, jnp.maximum))
        return carry

    lax.fori_loop(0, full, first, 0)
    s = logits(full)
    key_pos = full * block + lax.broadcasted_iota(jnp.int32, (tok, block), 1)
    query_pos = my_start + lax.broadcasted_iota(jnp.int32, (tok, block), 0)
    seen = key_pos <= query_pos
    s = jnp.where(seen[None], s.reshape(heads, tok, block), -1e30).reshape(s.shape)
    s_s[full] = s
    row_max = jnp.max(
        jnp.maximum(m_s[...], fold_lanes(s, jnp.maximum)), axis=1, keepdims=True
    )
    m_s[...] = jnp.broadcast_to(row_max, m_s.shape)

    p = jnp.exp2((ps_s[...] - m_s[:, :1]) * to_exp2)
    d = dot(do_s[...], pv_ref[...], NT)
    ps_s[...] = p
    pd_s[...] = d
    l_s[...] = fold_lanes(p, jnp.add)
    dl_s[...] = fold_lanes(p * d, jnp.add)

    def second(i, carry):
        d = dot(do_s[...], v_ref[pl.ds(pl.multiple_of(i * block, block), block), :], NT)
        p = jnp.exp2((s_s[i] - m_s[:, :1]) * to_exp2)
        s_s[i] = p
        d_s[i] = d
        l_s[...] += fold_lanes(p, jnp.add)
        dl_s[...] += fold_lanes(p * d, jnp.add)
        return carry

    lax.fori_loop(0, full + 1, second, 0)
    inverse = 1.0 / jnp.sum(l_s[...], axis=1, keepdims=True)
    delta = jnp.sum(dl_s[...], axis=1, keepdims=True) * inverse
    l_s[...] = jnp.broadcast_to(inverse, l_s.shape)
    dl_s[...] = jnp.broadcast_to(delta, dl_s.shape)
    acc_s[...] = jnp.zeros_like(acc_s)

    def third(i, carry):
        sg = (s_s[i] * (d_s[i] - dl_s[:, :1])).astype(jnp.bfloat16)
        acc_s[...] += dot(sg, k_ref[pl.ds(pl.multiple_of(i * block, block), block), :], NN)
        return carry

    lax.fori_loop(0, full + 1, third, 0)
    probs = ps_s[...] * l_s[:, :1]
    sg = (probs * (pd_s[...] - dl_s[:, :1])).astype(jnp.bfloat16)
    probs_b = probs.astype(jnp.bfloat16)
    dq = (acc_s[...] * l_s[...] + dot(sg, pk_ref[...], NN)) * scaling
    dq = dq.astype(jnp.bfloat16)
    for h in range(heads):
        dq_ref[:, h * HD : (h + 1) * HD] = dq[h * tok : (h + 1) * tok, :]
    kg = dot(sg, q_s[...], TN) * scaling
    vg = dot(probs_b, do_s[...], TN)

    @pl.when(pl.program_id(1) == 0)
    def _():
        kg_ref[...] = kg
        vg_ref[...] = vg

    @pl.when(pl.program_id(1) > 0)
    def _():
        kg_ref[...] += kg
        vg_ref[...] += vg


def attention(position, queries, out_grad, kv_all, prefix_kv):
    tok, q_width = queries.shape
    total, both = kv_all.shape
    heads_here = both // (2 * HD)
    group = QH // KVH
    per_tile = math.gcd(group, HEADS_PER_TILE)
    tiles = group // per_tile
    block = 2 * tok if total % (2 * tok) == 0 else tok
    rows = per_tile * tok
    prefix_len = prefix_kv.shape[0]
    row_block = pl.BlockSpec((tok, per_tile * HD), lambda g, j, pos: (0, g * tiles + j))
    key_block = pl.BlockSpec((total, HD), lambda g, j, pos: (0, g))
    value_block = pl.BlockSpec((total, HD), lambda g, j, pos: (0, heads_here + g))
    pk_block = pl.BlockSpec((prefix_len, HD), lambda g, j, pos: (0, g))
    pv_block = pl.BlockSpec((prefix_len, HD), lambda g, j, pos: (0, heads_here + g))
    f32 = jnp.float32
    return pl.pallas_call(
        attention_kernel,
        out_shape=(
            jax.ShapeDtypeStruct(queries.shape, jnp.bfloat16),
            jax.ShapeDtypeStruct((prefix_len, heads_here * HD), f32),
            jax.ShapeDtypeStruct((prefix_len, heads_here * HD), f32),
        ),
        grid_spec=pltpu.PrefetchScalarGridSpec(
            num_scalar_prefetch=1,
            grid=(heads_here, tiles),
            in_specs=[row_block, row_block, key_block, value_block, pk_block, pv_block],
            out_specs=(row_block, pk_block, pk_block),
            scratch_shapes=[
                pltpu.VMEM((rows, HD), jnp.bfloat16),
                pltpu.VMEM((rows, HD), jnp.bfloat16),
                pltpu.VMEM((total // block, rows, block), f32),
                pltpu.VMEM((total // block, rows, block), f32),
                pltpu.VMEM((rows, prefix_len), f32),
                pltpu.VMEM((rows, prefix_len), f32),
                pltpu.VMEM((rows, HD), f32),
                pltpu.VMEM((rows, HD), f32),
                pltpu.VMEM((rows, HD), f32),
                pltpu.VMEM((rows, HD), f32),
            ],
        ),
        compiler_params=pltpu.CompilerParams(vmem_limit_bytes=48 * 2**20),
    )(position, queries, out_grad, kv_all, kv_all, prefix_kv, prefix_kv)


def all_sum(value, axis):
    part = lax.psum_scatter(value, axis, scatter_dimension=0, tiled=True)
    return lax.all_gather(part.astype(jnp.bfloat16), axis, axis=0, tiled=True)


def on_device(prefix_embed, w_hidden, b_hidden, w_out, queries, keys, values, out_grad):
    columns = keys.shape[1]
    units = w_out.shape[0]
    kv_all = lax.all_gather(jnp.concatenate([keys, values], 1), "seq", axis=0, tiled=True)
    hidden_pre = jnp.dot(prefix_embed, w_hidden, preferred_element_type=jnp.float32) + b_hidden
    tangent = jnp.tanh(hidden_pre)
    hidden = tangent.astype(jnp.bfloat16)
    w_flat = w_out.reshape(units, 2 * columns)
    prefix_kv = all_sum(jnp.dot(hidden, w_flat, preferred_element_type=jnp.float32), "seq")
    position = lax.axis_index("seq").astype(jnp.int32).reshape(1)
    query_grad, key_grad, value_grad = attention(position, queries, out_grad, kv_all, prefix_kv)
    prefix_grads = all_sum(jnp.concatenate([key_grad, value_grad], 1), "seq")
    grad_w_out = dot(hidden, prefix_grads, TN).reshape(units, 2, columns)
    hidden_grad = lax.psum(dot(prefix_grads, w_flat, NT), "head")
    pre_grad = hidden_grad * (1.0 - tangent * tangent)
    pre_rounded = pre_grad.astype(jnp.bfloat16)
    grad_w_hidden = dot(prefix_embed, pre_rounded, TN)
    grad_b_hidden = jnp.sum(pre_grad, axis=0)
    grad_prefix = lax.psum(dot(pre_rounded, w_hidden, NT), "seq")
    return (query_grad, grad_w_out, grad_w_hidden, grad_b_hidden, grad_prefix)


def solution(mesh):
    placed = (
        P(),
        P(None, "seq"),
        P("seq"),
        P("seq", None, "head"),
        P("seq", "head"),
        P("seq", "head"),
        P("seq", "head"),
        P("seq", "head"),
    )
    return jax.shard_map(
        on_device,
        mesh=mesh,
        in_specs=placed,
        out_specs=(P("seq", "head"), P("seq", None, "head"), P(None, "seq"), P("seq"), P()),
        check_vma=False,
    )
```

time: 641 us -> 405 us (0.63)
  blocking collectives: 232 us -> 42.1 us
  waiting for transfers between devices: 192 us -> 300 us
  starting transfers between devices: 88.6 us -> 0.21 us
  local copies, waits for them, and re-layouts: 61.3 us -> 12.6 us
  Pallas kernels: 0 us -> 22.2 us
  matrix products: 28 us -> 8.14 us
  other arithmetic: 20.8 us -> 5.2 us
    psum x2 -> x0, blocking collectives: 232 us -> none  [the longest x1 157 us: on_device(): prefix_grads = lax.psum(both_grads, 'seq').astype(jnp.bfloat16)]
    reduce_scatter x0 -> x2, waiting for transfers between devices: none -> 158 us  [all_sum(): part = lax.psum_scatter(value, axis, scatter_dimension=0, tiled=True)]
    ppermute x15 -> x0, starting transfers between devices: 88.5 us -> none  [shifted(): lax.ppermute(value, axis, [(source, source + steps) for source in range(f...]
    psum x2, waiting for transfers between devices: 175 us -> 110 us  [the longest x1 84 us: on_device(): grad_prefix = lax.psum(dot(pre_rounded, w_hidden, NT), 'seq')]
    all_gather x0 -> x2, blocking collectives: none -> 42.1 us  [all_sum(): return lax.all_gather(part.astype(jnp.bfloat16), axis, axis=0, tiled=True)]
    all_gather x0 -> x1, waiting for transfers between devices: none -> 31.4 us  [on_device(): lax.all_gather(jnp.concatenate([keys, values], 1), 'seq', axis=0, tiled=T...]
    pallas_call x0 -> x1, Pallas kernels: none -> 22.2 us  [attention(): pl.pallas_call(attention_kernel, out_shape=(jax.ShapeDtypeStruct(queries....]
    dot_general x14 -> x5, matrix products: 26.2 us -> 7.7 us  [the longest x4 6.28 us: dot(): lax.dot_general(a, b, (dims, ((), ())), preferred_element_type=jnp.float32)]
  transfers between devices with their start and end apart: 17 -> 5, of which waited for: 17 -> 5; matrix products, arithmetic and copies ran while one was open for 3% -> 3% of each run, Pallas kernels for 0% -> 0%
where the time goes in v1:
time: 405 us; the launch traced here: 404 us
  waiting for transfers between devices  300 us (74%)
  blocking collectives  42.1 us (10%)
  Pallas kernels  22.2 us (5%)
  between operations  13.9 us (3%)
  local copies, waits for them, and re-layouts  12.6 us (3%)
  matrix products  8.14 us (2%)
  other arithmetic  5.2 us (1%)
    reduce_scatter x2, waiting for transfers between devices, all_sum(): part = lax.psum_scatter(value, axis, scatter_dimension=0, tiled=True)  158 us
    psum x1, waiting for transfers between devices, on_device(): grad_prefix = lax.psum(dot(pre_rounded, w_hidden, NT), 'seq')  84 us
    all_gather x2, blocking collectives, all_sum(): return lax.all_gather(part.astype(jnp.bfloat16), axis, axis=0, tiled=True)  42.1 us
    all_gather x1, waiting for transfers between devices, on_device(): lax.all_gather(jnp.concatenate([keys, values], 1), 'seq', axis=0, tiled=T...  31.4 us
    psum x1, waiting for transfers between devices, on_device(): hidden_grad = lax.psum(dot(prefix_grads, w_flat, NT), 'head')  25.9 us
    pallas_call x1, Pallas kernels, attention(): pl.pallas_call(attention_kernel, out_shape=(jax.ShapeDtypeStruct(queries....  22.2 us
    unnamed x23, local copies, waits for them, and re-layouts  8.52 us
  transfers between devices with their start and end apart: 5, of which 5 were waited for; matrix products, arithmetic and copies ran while one was open for 3% of the time, Pallas kernels for 0%

profile of v1, /device:TPU:0, one launch (start us, length us, event | category | flops | bytes accessed | tf_op | source)
XLA Modules:
  0.0 404.2 jit_solution(3088116649937395347)
XLA Ops:
  7.2 0.0 copy-start
  7.2 0.0 copy-start.5
  7.2 0.0 copy-start.9
  7.2 0.0 reduce-scatter.3.cloned.1.call-start
  7.2 1.6 copy.14
  8.8 0.0 copy-done
  8.8 0.0 copy-done.5
  8.8 0.0 copy-done.9
  8.9 0.0 copy-start.3
  8.9 0.4 fusion
  9.3 0.0 copy-start.7
  9.3 0.0 copy-start.8
  9.3 0.5 copy-done.3
  9.8 0.0 copy-start.1
  9.8 1.4 fusion.5
  11.2 0.0 reduce-scatter.3.cloned.1.call-update
  11.3 0.0 all-gather.2.cloned.1.call-start
  11.3 0.0 copy-done.7
  11.3 0.0 copy-done.8
  11.3 0.7 pad_maximum_fusion.1
  12.1 0.0 all-gather.2.cloned.1.call-update
  12.1 0.0 reduce-scatter.5.cloned.1.call-start
  12.1 60.2 %reduce-scatter.3.cloned.1.call-done = f32[16,1024]{1,0:T(8,128)} async-done(((f32[256,1024]{1,0:T(8,128)}), f32[16,1024]{1,0:T(8,128)}) %reduce-scatter.3.cloned.1.call-update) | async-done | bytes 65552 | tf_op jit(solution)/shard_map/reduce_scatter | solution.py:169
  72.4 0.8 convert_element_type.13
  73.2 21.3 %all_gather.10.pk_ref.pv_ref = bf16[256,1024]{1,0:T(8,128)(2,1)S(1)} all-gather(bf16[16,1024]{1,0:T(8,128)(2,1)S(1)} %convert_element_type.13), channel_id=1, replica_groups=mesh['seq'=16,'head'=2] {'seq'}, dimensions={0}, use_global_device_ids=true | all-gather | bytes 557056 | tf_op jit(solution)/shard_map/all_gather | solution.py:170
  94.5 31.4 %all-gather.2.cloned.1.call-done.k_ref.v_ref = bf16[2048,1024]{1,0:T(8,128)(2,1)} async-done(((bf16[128,1024]{1,0:T(8,128)(2,1)}), bf16[2048,1024]{1,0:T(8,128)(2,1)}) %all-gather.2.cloned.1.call-update) | async-done | bytes 4194320 | tf_op jit(solution)/shard_map/all_gather | solution.py:176
  125.9 0.0 copy-done.1
  126.0 0.0 copy-start.2
  126.0 1.2 copy-done.2
  127.2 22.2 %shard_map.119 = (bf16[128,4096]{1,0:T(8,128)(2,1)}, f32[256,512]{1,0:T(8,128)S(1)}, f32[256,512]{1,0:T(8,128)S(1)}) custom-call(s32[1]{0:T(128)} %bitcast.pos_ref, bf16[128,4096]{1,0:T(8,128)(2,1)S(1)} %copy-done.1, bf16[128,4096]{1,0:T(8,128)(2,1)S(1)} %copy-done.2, bf16[2048,1024]{1,0:T(8,128)(2,1)} %all-gather.2.cloned.1.call-done.k_ref.v_ref, ...), custom_call_target="tpu_custom_call" | custom-call | tf_op jit(solution)/shard_map/pallas_call | solution.py:139
  149.4 0.0 copy-start.4
  149.4 1.1 pad_maximum_fusion
  150.5 0.0 reduce-scatter.5.cloned.1.call-update
  150.5 0.0 all-reduce.3.cloned.1.call-start
  150.6 98.2 %reduce-scatter.5.cloned.1.call-done = f32[16,1024]{1,0:T(8,128)} async-done(((f32[256,1024]{1,0:T(8,128)}), f32[16,1024]{1,0:T(8,128)}) %reduce-scatter.5.cloned.1.call-update) | async-done | bytes 65552 | tf_op jit(solution)/shard_map/reduce_scatter | solution.py:169
  248.7 0.8 convert_element_type.14
  249.6 20.8 %all_gather.11 = bf16[256,1024]{1,0:T(8,128)(2,1)S(1)} all-gather(bf16[16,1024]{1,0:T(8,128)(2,1)S(1)} %convert_element_type.14), channel_id=1, replica_groups=mesh['seq'=16,'head'=2] {'seq'}, dimensions={0}, use_global_device_ids=true | all-gather | bytes 557056 | tf_op jit(solution)/shard_map/all_gather | solution.py:170
  270.4 0.0 copy-done.4
  270.4 1.3 fusion.7
  271.7 0.0 all-reduce.3.cloned.1.call-update
  271.7 0.0 all-reduce.5.cloned.1.call-start
  271.7 25.9 %all-reduce.3.cloned.1.call-done = f32[256,512]{1,0:T(8,128)} async-done(((f32[256,512]{1,0:T(8,128)}), f32[256,512]{1,0:T(8,128)}) %all-reduce.3.cloned.1.call-update) | async-done | bytes 524304 | tf_op jit(solution)/shard_map/psum | solution.py:186
  297.7 1.7 fusion.1
  299.4 1.4 fusion.8
  300.8 0.0 all-reduce.5.cloned.1.call-update
  300.9 1.8 fusion.3
  302.7 0.0 copy-start.6
  302.7 4.0 reshape.22
  306.7 0.0 copy-done.6
  306.7 1.8 convolution_bitcast_fusion
  308.5 2.9 copy.13
  311.4 84.0 %all-reduce.5.cloned.1.call-done = f32[256,1024]{1,0:T(8,128)} async-done(((f32[256,1024]{1,0:T(8,128)}), f32[256,1024]{1,0:T(8,128)}) %all-reduce.5.cloned.1.call-update) | async-done | bytes 1048592 | tf_op jit(solution)/shard_map/psum | solution.py:191
  395.4 2.3 copy.17
Async XLA Ops:
  7.2 1.7 copy-start
  7.2 1.7 copy-start.5
  7.2 1.7 copy-start.9
  7.2 65.2 %reduce-scatter.3.cloned.1.call-start = ((), (), s32[]{:S(2)}) async-start(), calls=%async_computation.3 | async-start | bytes 1114112 | tf_op jit(solution)/shard_map/reduce_scatter | solution.py:169
  8.9 1.0 copy-start.3
  9.3 2.0 copy-start.7
  9.3 2.0 copy-start.8
  9.8 116.1 %copy-start.1 = (bf16[128,4096]{1,0:T(8,128)(2,1)S(1)}, bf16[128,4096]{1,0:T(8,128)(2,1)}, u32[]{:S(2)}) copy-start(bf16[128,4096]{1,0:T(8,128)(2,1)} %q_ref.1) | copy-start | bytes 3145732
  11.3 114.7 %all-gather.2.cloned.1.call-start = ((), (), s32[]{:S(2)}) async-start(), calls=%async_computation.2 | async-start | bytes 4456448 | tf_op jit(solution)/shard_map/all_gather | solution.py:176
  12.1 236.6 %reduce-scatter.5.cloned.1.call-start = ((), (), s32[]{:S(2)}) async-start(), calls=%async_computation.4 | async-start | bytes 1114112 | tf_op jit(solution)/shard_map/reduce_scatter | solution.py:169
  126.0 1.2 copy-start.2
  149.4 121.0 %copy-start.4 = (bf16[64,8,2,512]{3,1,2,0:T(8,128)(2,1)S(1)}, bf16[64,8,2,512]{3,1,2,0:T(8,128)(2,1)}, u32[]{:S(2)}) copy-start(bf16[64,8,2,512]{3,1,2,0:T(8,128)(2,1)} %copy-done.3) | copy-start | bytes 3145732
  150.5 147.2 %all-reduce.3.cloned.1.call-start = ((), (), s32[]{:S(2)}) async-start(), calls=%async_computation.5 | async-start | bytes 1048576 | tf_op jit(solution)/shard_map/psum | solution.py:186
  271.7 123.7 %all-reduce.5.cloned.1.call-start = ((), (), s32[]{:S(2)}) async-start(), calls=%async_computation.6 | async-start | bytes 2097152 | tf_op jit(solution)/shard_map/psum | solution.py:191
  302.7 4.0 %copy-start.6 = (bf16[256,1024]{1,0:T(8,128)(2,1)S(1)}, bf16[256,1024]{1,0:T(8,128)(2,1)}, u32[]{:S(2)}) copy-start(bf16[256,1024]{1,0:T(8,128)(2,1)} %param.8) | copy-start | bytes 1572868
Sparse Core Ops, SparseCore 0:
  12.2 60.1 reduce-scatter.2
  75.4 50.5 all-gather.1
  150.6 98.0 reduce-scatter.4
  271.8 25.8 all-reduce.2
  302.0 93.3 all-reduce.4

commit v2 on v1

--- a/solution.py
+++ b/solution.py
@@ -30,7 +30,7 @@
 
 def attention_kernel(
     pos_ref, q_ref, do_ref, k_ref, v_ref, pk_ref, pv_ref,
-    dq_ref, kg_ref, vg_ref,
+    dq_ref, pg_ref,
     q_s, do_s, s_s, d_s, ps_s, pd_s, m_s, l_s, dl_s, acc_s,
 ):
     tok = q_ref.shape[0]
@@ -111,13 +111,13 @@
 
     @pl.when(pl.program_id(1) == 0)
     def _():
-        kg_ref[...] = kg
-        vg_ref[...] = vg
+        pg_ref[0] = kg
+        pg_ref[1] = vg
 
     @pl.when(pl.program_id(1) > 0)
     def _():
-        kg_ref[...] += kg
-        vg_ref[...] += vg
+        pg_ref[0] += kg
+        pg_ref[1] += vg
 
 
 def attention(position, queries, out_grad, kv_all, prefix_kv):
@@ -129,25 +129,25 @@
     tiles = group // per_tile
     block = 2 * tok if total % (2 * tok) == 0 else tok
     rows = per_tile * tok
-    prefix_len = prefix_kv.shape[0]
+    prefix_len = prefix_kv.shape[0] // 2
     row_block = pl.BlockSpec((tok, per_tile * HD), lambda g, j, pos: (0, g * tiles + j))
     key_block = pl.BlockSpec((total, HD), lambda g, j, pos: (0, g))
     value_block = pl.BlockSpec((total, HD), lambda g, j, pos: (0, heads_here + g))
     pk_block = pl.BlockSpec((prefix_len, HD), lambda g, j, pos: (0, g))
-    pv_block = pl.BlockSpec((prefix_len, HD), lambda g, j, pos: (0, heads_here + g))
+    pv_block = pl.BlockSpec((prefix_len, HD), lambda g, j, pos: (1, g))
+    pg_block = pl.BlockSpec((2, prefix_len, HD), lambda g, j, pos: (0, 0, g))
     f32 = jnp.float32
     return pl.pallas_call(
         attention_kernel,
         out_shape=(
             jax.ShapeDtypeStruct(queries.shape, jnp.bfloat16),
-            jax.ShapeDtypeStruct((prefix_len, heads_here * HD), f32),
-            jax.ShapeDtypeStruct((prefix_len, heads_here * HD), f32),
+            jax.ShapeDtypeStruct((2, prefix_len, heads_here * HD), f32),
         ),
         grid_spec=pltpu.PrefetchScalarGridSpec(
             num_scalar_prefetch=1,
             grid=(heads_here, tiles),
             in_specs=[row_block, row_block, key_block, value_block, pk_block, pv_block],
-            out_specs=(row_block, pk_block, pk_block),
+            out_specs=(row_block, pg_block),
             scratch_shapes=[
                 pltpu.VMEM((rows, HD), jnp.bfloat16),
                 pltpu.VMEM((rows, HD), jnp.bfloat16),
@@ -165,30 +165,137 @@
     )(position, queries, out_grad, kv_all, kv_all, prefix_kv, prefix_kv)
 
 
-def all_sum(value, axis):
-    part = lax.psum_scatter(value, axis, scatter_dimension=0, tiled=True)
-    return lax.all_gather(part.astype(jnp.bfloat16), axis, axis=0, tiled=True)
+MESH = pl.DeviceIdType.MESH
+
+
+def sum_kernel(levels, paired, x_ref, o_ref, *scratch):
+    recv, held = scratch[:levels], scratch[levels : 2 * levels]
+    send_sem, recv_sem = scratch[2 * levels :]
+    me = lax.axis_index("seq")
+    bits = [(me // 2**k) % 2 for k in range(levels)]
+    partners = [me + 2**k * (1 - 2 * bits[k]) for k in range(levels)]
+    barrier = pltpu.get_barrier_semaphore()
+    for partner in partners:
+        pl.semaphore_signal(barrier, inc=1, device_id={"seq": partner}, device_id_type=MESH)
+    if paired:
+        head = lax.axis_index("head")
+        other = 1 - head
+        pl.semaphore_signal(barrier, inc=1, device_id={"head": other}, device_id_type=MESH)
+    pl.semaphore_wait(barrier, levels + (1 if paired else 0))
+
+    rows = x_ref.shape[0]
+    source = x_ref
+    copies = []
+    starts = []
+    start = 0
+    for k in range(levels):
+        half = rows // 2 ** (k + 1)
+        copy = pltpu.make_async_remote_copy(
+            src_ref=source.at[pl.ds(pl.multiple_of((1 - bits[k]) * half, half), half)],
+            dst_ref=recv[k],
+            send_sem=send_sem.at[k],
+            recv_sem=recv_sem.at[k],
+            device_id={"seq": partners[k]},
+            device_id_type=MESH,
+        )
+        copy.start()
+        copy.wait_recv()
+        held[k][...] = source[pl.ds(pl.multiple_of(bits[k] * half, half), half), :] + recv[k][...]
+        source = held[k]
+        copies.append(copy)
+        start = start + bits[k] * half
+        starts.append(start)
+    out = o_ref.at[head] if paired else o_ref.at[0]
+    last = rows // 2**levels
+    out[pl.ds(pl.multiple_of(start, last), last), :] = source[...].astype(o_ref.dtype)
+    for k in reversed(range(levels)):
+        half = rows // 2 ** (k + 1)
+        part = out.at[pl.ds(pl.multiple_of(starts[k], half), half)]
+        copy = pltpu.make_async_remote_copy(
+            src_ref=part,
+            dst_ref=part,
+            send_sem=send_sem.at[levels + k],
+            recv_sem=recv_sem.at[levels + k],
+            device_id={"seq": partners[k]},
+            device_id_type=MESH,
+        )
+        copy.start()
+        copy.wait_recv()
+        copies.append(copy)
+    if paired:
+        copy = pltpu.make_async_remote_copy(
+            src_ref=out,
+            dst_ref=out,
+            send_sem=send_sem.at[2 * levels],
+            recv_sem=recv_sem.at[2 * levels],
+            device_id={"head": other},
+            device_id_type=MESH,
+        )
+        copy.start()
+        copy.wait_recv()
+        copies.append(copy)
+    for copy in copies:
+        copy.wait_send()
+
+
+def all_sum(value, collective_id, paired=False):
+    rows, columns = value.shape
+    levels = lax.axis_size("seq").bit_length() - 1
+    shapes = [pltpu.VMEM((rows // 2 ** (k + 1), columns), jnp.float32) for k in range(levels)]
+    return pl.pallas_call(
+        functools.partial(sum_kernel, levels, paired),
+        out_shape=jax.ShapeDtypeStruct((2 if paired else 1, rows, columns), jnp.bfloat16),
+        in_specs=[pl.BlockSpec(memory_space=pltpu.VMEM)],
+        out_specs=pl.BlockSpec(memory_space=pltpu.VMEM),
+        scratch_shapes=shapes
+        + shapes
+        + [
+            pltpu.SemaphoreType.DMA((2 * levels + 1,)),
+            pltpu.SemaphoreType.DMA((2 * levels + 1,)),
+        ],
+        compiler_params=pltpu.CompilerParams(
+            collective_id=collective_id, has_side_effects=True, vmem_limit_bytes=24 * 2**20
+        ),
+    )(value)
 
 
 def on_device(prefix_embed, w_hidden, b_hidden, w_out, queries, keys, values, out_grad):
     columns = keys.shape[1]
-    units = w_out.shape[0]
+    emb = w_hidden.shape[0]
+    prefix_len = prefix_embed.shape[0]
     kv_all = lax.all_gather(jnp.concatenate([keys, values], 1), "seq", axis=0, tiled=True)
     hidden_pre = jnp.dot(prefix_embed, w_hidden, preferred_element_type=jnp.float32) + b_hidden
     tangent = jnp.tanh(hidden_pre)
     hidden = tangent.astype(jnp.bfloat16)
-    w_flat = w_out.reshape(units, 2 * columns)
-    prefix_kv = all_sum(jnp.dot(hidden, w_flat, preferred_element_type=jnp.float32), "seq")
+    w_key, w_value = w_out[:, 0], w_out[:, 1]
+    partial_kv = jnp.concatenate([dot(hidden, w_key, NN), dot(hidden, w_value, NN)], 0)
+    prefix_kv = all_sum(partial_kv, 0)[0]
     position = lax.axis_index("seq").astype(jnp.int32).reshape(1)
-    query_grad, key_grad, value_grad = attention(position, queries, out_grad, kv_all, prefix_kv)
-    prefix_grads = all_sum(jnp.concatenate([key_grad, value_grad], 1), "seq")
-    grad_w_out = dot(hidden, prefix_grads, TN).reshape(units, 2, columns)
-    hidden_grad = lax.psum(dot(prefix_grads, w_flat, NT), "head")
+    query_grad, both_grads = attention(position, queries, out_grad, kv_all, prefix_kv)
+    prefix_grads = all_sum(both_grads.reshape(2 * prefix_len, columns), 1)[0]
+    pg_key, pg_value = prefix_grads[:prefix_len], prefix_grads[prefix_len:]
+    hidden_part = dot(pg_key, w_key, NT) + dot(pg_value, w_value, NT)
+    if lax.axis_size("head") == 2:
+        hidden_grad = hidden_part + lax.ppermute(hidden_part, "head", [(0, 1), (1, 0)])
+    else:
+        hidden_grad = lax.psum(hidden_part, "head")
+    grad_w_out = jnp.stack([dot(hidden, pg_key, TN), dot(hidden, pg_value, TN)], 1)
     pre_grad = hidden_grad * (1.0 - tangent * tangent)
     pre_rounded = pre_grad.astype(jnp.bfloat16)
+    paired = lax.axis_size("head") == 2 and emb % 512 == 0
+    share = emb // 2 if paired else emb
+    if paired:
+        w_share = lax.dynamic_slice_in_dim(w_hidden, lax.axis_index("head") * share, share, 0)
+    else:
+        w_share = w_hidden
+    low = dot(pre_rounded, w_share[: share // 2], NT)
+    high = dot(pre_rounded, w_share[share // 2 :], NT)
+    summed = all_sum(jnp.concatenate([low, high], 0), 2, paired)
     grad_w_hidden = dot(prefix_embed, pre_rounded, TN)
     grad_b_hidden = jnp.sum(pre_grad, axis=0)
-    grad_prefix = lax.psum(dot(pre_rounded, w_hidden, NT), "seq")
+    summed = summed.reshape(-1, prefix_len, share // 2)
+    grad_prefix = jnp.concatenate([summed[i] for i in range(summed.shape[0])], 1)
+    grad_prefix = grad_prefix.astype(jnp.float32)
     return (query_grad, grad_w_out, grad_w_hidden, grad_b_hidden, grad_prefix)
 
 

time: 405 us -> 227 us (0.56)
  waiting for transfers between devices: 300 us -> 19.1 us
  Pallas kernels: 22.2 us -> 171 us
  blocking collectives: 42.1 us -> 0 us
    reduce_scatter x2 -> x0, waiting for transfers between devices: 158 us -> none  [all_sum(): part = lax.psum_scatter(value, axis, scatter_dimension=0, tiled=True)]
    pallas_call x0 -> x3, Pallas kernels: none -> 149 us  [all_sum(): pl.pallas_call(functools.partial(sum_kernel, levels, paired), out_shape=j...]
    psum x2 -> x0, waiting for transfers between devices: 110 us -> none  [the longest x1 84 us: on_device(): grad_prefix = lax.psum(dot(pre_rounded, w_hidden, NT), 'seq')]
    all_gather x2 -> x0, blocking collectives: 42.1 us -> none  [all_sum(): return lax.all_gather(part.astype(jnp.bfloat16), axis, axis=0, tiled=True)]
    all_gather x1, waiting for transfers between devices: 31.4 us -> 9.99 us  [on_device(): lax.all_gather(jnp.concatenate([keys, values], 1), 'seq', axis=0, tiled=T...]
    ppermute x0 -> x1, waiting for transfers between devices: none -> 9.05 us  [on_device(): lax.ppermute(hidden_part, 'head', [(0, 1), (1, 0)])]
    unnamed x23 -> x22, local copies, waits for them, and re-layouts: 8.52 us -> 6.68 us
  transfers between devices with their start and end apart: 5 -> 2, of which waited for: 5 -> 2; matrix products, arithmetic and copies ran while one was open for 3% -> 4% of each run, Pallas kernels for 0% -> 20%
where the time goes in v2:
time: 227 us; the launch traced here: 226 us
  Pallas kernels  171 us (75%)
  waiting for transfers between devices  19.1 us (8%)
  between operations  14.2 us (6%)
  local copies, waits for them, and re-layouts  8.86 us (4%)
  other arithmetic  5.86 us (3%)
  matrix products  5.21 us (2%)
    pallas_call x3, Pallas kernels, all_sum(): pl.pallas_call(functools.partial(sum_kernel, levels, paired), out_shape=j...  149 us
    pallas_call x1, Pallas kernels, attention(): pl.pallas_call(attention_kernel, out_shape=(jax.ShapeDtypeStruct(queries....  22.3 us
    all_gather x1, waiting for transfers between devices, on_device(): lax.all_gather(jnp.concatenate([keys, values], 1), 'seq', axis=0, tiled=T...  9.99 us
    ppermute x1, waiting for transfers between devices, on_device(): lax.ppermute(hidden_part, 'head', [(0, 1), (1, 0)])  9.05 us
    unnamed x22, local copies, waits for them, and re-layouts  6.68 us
  transfers between devices with their start and end apart: 2, of which 2 were waited for; matrix products, arithmetic and copies ran while one was open for 4% of the time, Pallas kernels for 20%

profile of v2, /device:TPU:0, one launch (start us, length us, event | category | flops | bytes accessed | tf_op | source)
XLA Modules:
  0.0 225.7 jit_solution(10198209258710077970)
XLA Ops:
  7.2 0.0 copy-start
  7.2 0.0 copy-start.3
  7.2 0.0 all-gather.2.cloned.1.call-start
  7.2 1.8 pad_maximum_fusion.3
  9.1 0.0 all-gather.2.cloned.1.call-update
  9.1 0.0 copy-done
  9.1 2.3 %fusion.23 = (bf16[256,512]{1,0:T(8,128)(2,1)S(1)}, f32[256,512]{1,0:T(8,128)}) fusion(f32[512]{0:T(512)} %param.10, bf16[256,1024]{1,0:T(8,128)(2,1)} %param.8, bf16[1024,512]{1,0:T(8,128)(2,1)S(1)} %copy-done), kind=kOutput, calls=%fused_computation.40 | convolution fusion | flops 268697600 | bytes 2361344 | tf_op jit(solution)/shard_map/dot_general | solution.py:267
  11.4 0.0 copy-done.3
  11.4 1.5 fusion.22
  12.9 0.0 copy-start.4
  12.9 0.0 copy-start.6
  12.9 0.3 fusion.14
  13.2 0.3 fusion.15
  13.5 0.3 copy-done.4
  13.9 0.3 copy-done.6
  14.2 0.0 copy-start.1
  14.2 0.1 pad_maximum_fusion.1.x_ref
  14.3 45.9 %shard_map.119 = bf16[1,512,512]{2,1,0:T(8,128)(2,1)S(1)} custom-call(f32[512,512]{1,0:T(8,128)S(1)} %pad_maximum_fusion.1.x_ref), custom_call_target="tpu_custom_call" | custom-call | tf_op jit(solution)/shard_map/pallas_call | solution.py:245
  60.2 10.0 %all-gather.2.cloned.1.call-done.k_ref.v_ref = bf16[2048,1024]{1,0:T(8,128)(2,1)} async-done(((bf16[128,1024]{1,0:T(8,128)(2,1)}), bf16[2048,1024]{1,0:T(8,128)(2,1)}) %all-gather.2.cloned.1.call-update) | async-done | bytes 4194320 | tf_op jit(solution)/shard_map/all_gather | solution.py:266
  70.1 0.0 copy-done.1
  70.1 0.0 copy-start.2
  70.1 1.2 copy-done.2
  71.4 0.0 copy-start.7
  71.4 22.3 %shard_map.120 = (bf16[128,4096]{1,0:T(8,128)(2,1)}, f32[2,256,512]{2,1,0:T(8,128)S(1)}) custom-call(s32[1]{0:T(128)} %bitcast.pos_ref, bf16[128,4096]{1,0:T(8,128)(2,1)S(1)} %copy-done.1, bf16[128,4096]{1,0:T(8,128)(2,1)S(1)} %copy-done.2, bf16[2048,1024]{1,0:T(8,128)(2,1)} %all-gather.2.cloned.1.call-done.k_ref.v_ref, ...), custom_call_target="tpu_custom_call" | custom-call | tf_op jit(solution)/shard_map/pallas_call | solution.py:140
  93.7 0.0 copy-start.5
  93.7 69.6 %shard_map.121 = bf16[1,512,512]{2,1,0:T(8,128)(2,1)S(1)} custom-call(f32[512,512]{1,0:T(8,128)S(1)} %bitcast.49), custom_call_target="tpu_custom_call" | custom-call | tf_op jit(solution)/shard_map/pallas_call | solution.py:245
  163.2 0.0 copy-done.7
  163.2 0.3 fusion.7
  163.6 0.0 copy-done.5
  163.6 0.3 convolution_add_fusion.1
  163.9 1.6 collective-permute-start
  165.5 0.3 convolution_bitcast_fusion.2
  165.8 0.3 convolution_bitcast_fusion.1
  166.1 0.2 pad_maximum_fusion
  166.3 0.0 copy-start.9
  166.3 2.9 %copy.17 = f32[512,2,512]{2,1,0:T(2,128)} copy(f32[512,2,512]{2,0,1:T(8,128)S(1)} %pad_maximum_fusion) | data formatting | bytes 4194304
  169.3 0.0 copy-start.8
  169.3 9.0 %collective-permute-done = f32[256,512]{1,0:T(8,128)} collective-permute-done((f32[256,512]{1,0:T(8,128)S(1)}, f32[256,512]{1,0:T(8,128)}, u32[]{:S(2)}, u32[]{:S(2)}) %collective-permute-start) | collective-permute-done | bytes 524320 | tf_op jit(solution)/shard_map/ppermute | solution.py:279
  178.3 0.0 copy-done.9
  178.3 1.8 fusion.21
  180.1 0.3 fusion.3
  180.4 0.0 copy-done.8
  180.4 0.5 convolution_bitcast_fusion
  180.8 0.3 fusion.1
  181.1 33.2 %shard_map.122 = bf16[2,512,256]{2,1,0:T(8,128)(2,1)S(1)} custom-call(f32[512,256]{1,0:T(8,128)S(1)} %pad_maximum_fusion.2.x_ref), custom_call_target="tpu_custom_call" | custom-call | tf_op jit(solution)/shard_map/pallas_call | solution.py:245
  214.3 0.7 slice_bitcast_fusion.3
  215.0 1.8 copy.18
  216.8 2.0 maximum_convert_fusion
  (1 shorter events, 0.0 us)
Async XLA Ops:
  7.2 1.9 copy-start
  7.2 4.2 %copy-start.3 = (bf16[512,2,512]{2,1,0:T(2,128)(2,1)S(1)}, bf16[512,2,512]{2,1,0:T(2,128)(2,1)}, u32[]{:S(2)}) copy-start(bf16[512,2,512]{2,1,0:T(2,128)(2,1)} %param.11) | copy-start | bytes 3145732
  7.2 63.0 %all-gather.2.cloned.1.call-start = ((), (), s32[]{:S(2)}) async-start(), calls=%async_computation | async-start | bytes 4456448 | tf_op jit(solution)/shard_map/all_gather | solution.py:266
  12.9 1.0 copy-start.4
  12.9 1.3 copy-start.6
  14.2 55.9 %copy-start.1 = (bf16[128,4096]{1,0:T(8,128)(2,1)S(1)}, bf16[128,4096]{1,0:T(8,128)(2,1)}, u32[]{:S(2)}) copy-start(bf16[128,4096]{1,0:T(8,128)(2,1)} %q_ref.1) | copy-start | bytes 3145732
  70.1 1.2 copy-start.2
  71.4 91.9 %copy-start.7 = (bf16[512,1,512]{2,1,0:T(2,128)(2,1)S(1)}, bf16[512,1,512]{2,1,0:T(2,128)(2,1)}, u32[]{:S(2)}) copy-start(bf16[512,1,512]{2,1,0:T(2,128)(2,1)} %copy-done.6) | copy-start | bytes 1572868
  93.7 69.9 %copy-start.5 = (bf16[512,1,512]{2,1,0:T(2,128)(2,1)S(1)}, bf16[512,1,512]{2,1,0:T(2,128)(2,1)}, u32[]{:S(2)}) copy-start(bf16[512,1,512]{2,1,0:T(2,128)(2,1)} %copy-done.4) | copy-start | bytes 1572868
  163.9 14.4 %collective-permute-start = (f32[256,512]{1,0:T(8,128)S(1)}, f32[256,512]{1,0:T(8,128)}, u32[]{:S(2)}, u32[]{:S(2)}) collective-permute-start(f32[256,512]{1,0:T(8,128)S(1)} %convolution_add_fusion.1), channel_id=1, source_target_pairs={{0,1},{1,0},{2,3},{3,2},{4,5},{5,4},{6,7},{7,6},{8,9},{9,8},{10,11... | collective-permute-start | bytes 1572872 | tf_op jit(solution)/shard_map/ppermute | solution.py:279
  166.3 12.0 %copy-start.9 = (f32[256,512]{1,0:T(8,128)S(1)}, f32[256,512]{1,0:T(8,128)}, u32[]{:S(2)}) copy-start(f32[256,512]{1,0:T(8,128)} %get-tuple-element.28) | copy-start | bytes 1572868
  169.3 11.1 %copy-start.8 = (bf16[256,1024]{1,0:T(8,128)(2,1)S(1)}, bf16[256,1024]{1,0:T(8,128)(2,1)}, u32[]{:S(2)}) copy-start(bf16[256,1024]{1,0:T(8,128)(2,1)} %param.8) | copy-start | bytes 1572868
Sparse Core Ops, SparseCore 0:
  10.8 59.3 all-gather.1

commit v3 on v2

--- a/solution.py
+++ b/solution.py
@@ -11,7 +11,7 @@
 QH = 64
 KVH = 8
 HD = 128
-HEADS_PER_TILE = 4
+HEADS_PER_TILE = 8
 
 
 def dot(a, b, dims):
@@ -26,6 +26,10 @@
 def fold_lanes(block, op):
     parts = [block[:, i : i + HD] for i in range(0, block.shape[1], HD)]
     return functools.reduce(op, parts)
+
+
+def widen(rows, width):
+    return jnp.concatenate([rows] * (width // HD), axis=1)
 
 
 def attention_kernel(
@@ -70,7 +74,7 @@
     )
     m_s[...] = jnp.broadcast_to(row_max, m_s.shape)
 
-    p = jnp.exp2((ps_s[...] - m_s[:, :1]) * to_exp2)
+    p = jnp.exp2((ps_s[...] - widen(m_s[...], ps_s.shape[1])) * to_exp2)
     d = dot(do_s[...], pv_ref[...], NT)
     ps_s[...] = p
     pd_s[...] = d
@@ -79,7 +83,7 @@
 
     def second(i, carry):
         d = dot(do_s[...], v_ref[pl.ds(pl.multiple_of(i * block, block), block), :], NT)
-        p = jnp.exp2((s_s[i] - m_s[:, :1]) * to_exp2)
+        p = jnp.exp2((s_s[i] - widen(m_s[...], block)) * to_exp2)
         s_s[i] = p
         d_s[i] = d
         l_s[...] += fold_lanes(p, jnp.add)
@@ -94,13 +98,13 @@
     acc_s[...] = jnp.zeros_like(acc_s)
 
     def third(i, carry):
-        sg = (s_s[i] * (d_s[i] - dl_s[:, :1])).astype(jnp.bfloat16)
+        sg = (s_s[i] * (d_s[i] - widen(dl_s[...], block))).astype(jnp.bfloat16)
         acc_s[...] += dot(sg, k_ref[pl.ds(pl.multiple_of(i * block, block), block), :], NN)
         return carry
 
     lax.fori_loop(0, full + 1, third, 0)
-    probs = ps_s[...] * l_s[:, :1]
-    sg = (probs * (pd_s[...] - dl_s[:, :1])).astype(jnp.bfloat16)
+    probs = ps_s[...] * widen(l_s[...], ps_s.shape[1])
+    sg = (probs * (pd_s[...] - widen(dl_s[...], pd_s.shape[1]))).astype(jnp.bfloat16)
     probs_b = probs.astype(jnp.bfloat16)
     dq = (acc_s[...] * l_s[...] + dot(sg, pk_ref[...], NN)) * scaling
     dq = dq.astype(jnp.bfloat16)
@@ -168,9 +172,12 @@
 MESH = pl.DeviceIdType.MESH
 
 
-def sum_kernel(levels, paired, x_ref, o_ref, *scratch):
-    recv, held = scratch[:levels], scratch[levels : 2 * levels]
-    send_sem, recv_sem = scratch[2 * levels :]
+def sum_kernel(levels, orders, paired, x_ref, o_ref, *scratch):
+    chunks = range(len(orders))
+    recv = [scratch[c * levels : (c + 1) * levels] for c in chunks]
+    scratch = scratch[len(orders) * levels :]
+    held = [scratch[c * levels : (c + 1) * levels] for c in chunks]
+    send_sem, recv_sem = scratch[len(orders) * levels :]
     me = lax.axis_index("seq")
     bits = [(me // 2**k) % 2 for k in range(levels)]
     partners = [me + 2**k * (1 - 2 * bits[k]) for k in range(levels)]
@@ -184,50 +191,67 @@
     pl.semaphore_wait(barrier, levels + (1 if paired else 0))
 
     rows = x_ref.shape[0]
-    source = x_ref
+    width = x_ref.shape[1] // len(orders)
+    out = o_ref.at[head] if paired else o_ref.at[0]
+    source = [x_ref.at[:, pl.ds(c * width, width)] for c in chunks]
     copies = []
-    starts = []
-    start = 0
-    for k in range(levels):
-        half = rows // 2 ** (k + 1)
-        copy = pltpu.make_async_remote_copy(
-            src_ref=source.at[pl.ds(pl.multiple_of((1 - bits[k]) * half, half), half)],
-            dst_ref=recv[k],
-            send_sem=send_sem.at[k],
-            recv_sem=recv_sem.at[k],
-            device_id={"seq": partners[k]},
-            device_id_type=MESH,
-        )
-        copy.start()
-        copy.wait_recv()
-        held[k][...] = source[pl.ds(pl.multiple_of(bits[k] * half, half), half), :] + recv[k][...]
-        source = held[k]
-        copies.append(copy)
-        start = start + bits[k] * half
-        starts.append(start)
-    out = o_ref.at[head] if paired else o_ref.at[0]
+    starts = [[] for c in chunks]
+    start = [0 for c in chunks]
+    for step in range(levels):
+        half = rows // 2 ** (step + 1)
+        going = []
+        for c in chunks:
+            k = orders[c][step]
+            copy = pltpu.make_async_remote_copy(
+                src_ref=source[c].at[pl.ds(pl.multiple_of((1 - bits[k]) * half, half), half)],
+                dst_ref=recv[c][step],
+                send_sem=send_sem.at[c, step],
+                recv_sem=recv_sem.at[c, step],
+                device_id={"seq": partners[k]},
+                device_id_type=MESH,
+            )
+            copy.start()
+            going.append(copy)
+        for c in chunks:
+            k = orders[c][step]
+            going[c].wait_recv()
+            kept = source[c][pl.ds(pl.multiple_of(bits[k] * half, half), half), :]
+            held[c][step][...] = kept + recv[c][step][...]
+            source[c] = held[c][step]
+            start[c] = start[c] + bits[k] * half
+            starts[c].append(start[c])
+        copies += going
     last = rows // 2**levels
-    out[pl.ds(pl.multiple_of(start, last), last), :] = source[...].astype(o_ref.dtype)
-    for k in reversed(range(levels)):
-        half = rows // 2 ** (k + 1)
-        part = out.at[pl.ds(pl.multiple_of(starts[k], half), half)]
-        copy = pltpu.make_async_remote_copy(
-            src_ref=part,
-            dst_ref=part,
-            send_sem=send_sem.at[levels + k],
-            recv_sem=recv_sem.at[levels + k],
-            device_id={"seq": partners[k]},
-            device_id_type=MESH,
-        )
-        copy.start()
-        copy.wait_recv()
-        copies.append(copy)
+    for c in chunks:
+        out[pl.ds(pl.multiple_of(start[c], last), last), pl.ds(c * width, width)] = source[c][
+            ...
+        ].astype(o_ref.dtype)
+    for step in reversed(range(levels)):
+        half = rows // 2 ** (step + 1)
+        going = []
+        for c in chunks:
+            part = out.at[
+                pl.ds(pl.multiple_of(starts[c][step], half), half), pl.ds(c * width, width)
+            ]
+            copy = pltpu.make_async_remote_copy(
+                src_ref=part,
+                dst_ref=part,
+                send_sem=send_sem.at[c, levels + step],
+                recv_sem=recv_sem.at[c, levels + step],
+                device_id={"seq": partners[orders[c][step]]},
+                device_id_type=MESH,
+            )
+            copy.start()
+            going.append(copy)
+        for copy in going:
+            copy.wait_recv()
+        copies += going
     if paired:
         copy = pltpu.make_async_remote_copy(
             src_ref=out,
             dst_ref=out,
-            send_sem=send_sem.at[2 * levels],
-            recv_sem=recv_sem.at[2 * levels],
+            send_sem=send_sem.at[0, 2 * levels],
+            recv_sem=recv_sem.at[0, 2 * levels],
             device_id={"head": other},
             device_id_type=MESH,
         )
@@ -241,17 +265,20 @@
 def all_sum(value, collective_id, paired=False):
     rows, columns = value.shape
     levels = lax.axis_size("seq").bit_length() - 1
-    shapes = [pltpu.VMEM((rows // 2 ** (k + 1), columns), jnp.float32) for k in range(levels)]
+    orders = [list(range(levels))]
+    if columns % (2 * HD) == 0 and levels > 2:
+        orders.append([0] + list(range(2, levels)) + [1])
+    width = columns // len(orders)
+    shapes = [pltpu.VMEM((rows // 2 ** (k + 1), width), jnp.float32) for k in range(levels)]
     return pl.pallas_call(
-        functools.partial(sum_kernel, levels, paired),
+        functools.partial(sum_kernel, levels, orders, paired),
         out_shape=jax.ShapeDtypeStruct((2 if paired else 1, rows, columns), jnp.bfloat16),
         in_specs=[pl.BlockSpec(memory_space=pltpu.VMEM)],
         out_specs=pl.BlockSpec(memory_space=pltpu.VMEM),
-        scratch_shapes=shapes
-        + shapes
+        scratch_shapes=shapes * (2 * len(orders))
         + [
-            pltpu.SemaphoreType.DMA((2 * levels + 1,)),
-            pltpu.SemaphoreType.DMA((2 * levels + 1,)),
+            pltpu.SemaphoreType.DMA((len(orders), 2 * levels + 1)),
+            pltpu.SemaphoreType.DMA((len(orders), 2 * levels + 1)),
         ],
         compiler_params=pltpu.CompilerParams(
             collective_id=collective_id, has_side_effects=True, vmem_limit_bytes=24 * 2**20
@@ -276,7 +303,9 @@
     pg_key, pg_value = prefix_grads[:prefix_len], prefix_grads[prefix_len:]
     hidden_part = dot(pg_key, w_key, NT) + dot(pg_value, w_value, NT)
     if lax.axis_size("head") == 2:
-        hidden_grad = hidden_part + lax.ppermute(hidden_part, "head", [(0, 1), (1, 0)])
+        mine = hidden_part.astype(jnp.bfloat16)
+        theirs = lax.ppermute(mine, "head", [(0, 1), (1, 0)])
+        hidden_grad = mine.astype(jnp.float32) + theirs.astype(jnp.float32)
     else:
         hidden_grad = lax.psum(hidden_part, "head")
     grad_w_out = jnp.stack([dot(hidden, pg_key, TN), dot(hidden, pg_value, TN)], 1)

time: 227 us -> 190 us (0.84)
  Pallas kernels: 171 us -> 137 us
    pallas_call x3, Pallas kernels: 149 us -> 125 us  [all_sum(): pl.pallas_call(functools.partial(sum_kernel, levels, orders, paired), out...]
    pallas_call x1, Pallas kernels: 22.3 us -> 12.2 us  [attention(): pl.pallas_call(attention_kernel, out_shape=(jax.ShapeDtypeStruct(queries....]
    ppermute x1, waiting for transfers between devices: 9.05 us -> 3.81 us  [on_device(): theirs = lax.ppermute(mine, 'head', [(0, 1), (1, 0)])]
    all_gather x1, waiting for transfers between devices: 9.99 us -> 14.9 us  [on_device(): lax.all_gather(jnp.concatenate([keys, values], 1), 'seq', axis=0, tiled=T...]
    unnamed x22 -> x20, local copies, waits for them, and re-layouts: 6.68 us -> 6.68 us
  transfers between devices with their start and end apart: 2 -> 2, of which waited for: 2 -> 2; matrix products, arithmetic and copies ran while one was open for 4% -> 4% of each run, Pallas kernels for 20% -> 21%
where the time goes in v3:
time: 190 us
  Pallas kernels  137 us (72%)
  waiting for transfers between devices  18.7 us (10%)
  between operations  14.2 us (7%)
  local copies, waits for them, and re-layouts  8.88 us (5%)
  other arithmetic  4.88 us (3%)
  matrix products  4.4 us (2%)
    pallas_call x3, Pallas kernels, all_sum(): pl.pallas_call(functools.partial(sum_kernel, levels, orders, paired), out...  125 us
    all_gather x1, waiting for transfers between devices, on_device(): lax.all_gather(jnp.concatenate([keys, values], 1), 'seq', axis=0, tiled=T...  14.9 us
    pallas_call x1, Pallas kernels, attention(): pl.pallas_call(attention_kernel, out_shape=(jax.ShapeDtypeStruct(queries....  12.2 us
    unnamed x20, local copies, waits for them, and re-layouts  6.68 us
    ppermute x1, waiting for transfers between devices, on_device(): theirs = lax.ppermute(mine, 'head', [(0, 1), (1, 0)])  3.81 us
  transfers between devices with their start and end apart: 2, of which 2 were waited for; matrix products, arithmetic and copies ran while one was open for 4% of the time, Pallas kernels for 21%

profile of v3, /device:TPU:0, one launch (start us, length us, event | category | flops | bytes accessed | tf_op | source)
XLA Modules:
  0.0 189.6 jit_solution(5665406878631626334)
XLA Ops:
  7.2 0.0 copy-start
  7.2 0.0 copy-start.3
  7.2 0.0 all-gather.2.cloned.1.call-start
  7.2 1.8 pad_maximum_fusion.3
  9.1 0.0 all-gather.2.cloned.1.call-update
  9.1 0.0 copy-done
  9.1 1.5 fusion.22
  10.6 0.0 copy-done.3
  10.6 1.5 fusion.21
  12.1 0.0 copy-start.4
  12.1 0.0 copy-start.6
  12.2 0.3 fusion.15
  12.5 0.3 fusion.16
  12.8 0.3 copy-done.4
  13.1 0.3 copy-done.6
  13.4 0.0 copy-start.1
  13.4 0.1 pad_maximum_fusion.1.x_ref
  13.5 39.2 %shard_map.119 = bf16[1,512,512]{2,1,0:T(8,128)(2,1)S(1)} custom-call(f32[512,512]{1,0:T(8,128)S(1)} %pad_maximum_fusion.1.x_ref), custom_call_target="tpu_custom_call" | custom-call | tf_op jit(solution)/shard_map/pallas_call | solution.py:273
  52.8 14.9 %all-gather.2.cloned.1.call-done.k_ref.v_ref = bf16[2048,1024]{1,0:T(8,128)(2,1)} async-done(((bf16[128,1024]{1,0:T(8,128)(2,1)}), bf16[2048,1024]{1,0:T(8,128)(2,1)}) %all-gather.2.cloned.1.call-update) | async-done | bytes 4194320 | tf_op jit(solution)/shard_map/all_gather | solution.py:293
  67.7 0.0 copy-done.1
  67.7 0.0 copy-start.2
  67.7 1.2 copy-done.2
  68.9 0.0 copy-start.7
  68.9 12.2 %shard_map.120 = (bf16[128,4096]{1,0:T(8,128)(2,1)}, f32[2,256,512]{2,1,0:T(8,128)S(1)}) custom-call(s32[1]{0:T(128)} %bitcast.pos_ref, bf16[128,4096]{1,0:T(8,128)(2,1)S(1)} %copy-done.1, bf16[128,4096]{1,0:T(8,128)(2,1)S(1)} %copy-done.2, bf16[2048,1024]{1,0:T(8,128)(2,1)} %all-gather.2.cloned.1.call-done.k_ref.v_ref, ...), custom_call_target="tpu_custom_call" | custom-call | tf_op jit(solution)/shard_map/pallas_call | solution.py:144
  81.1 0.0 copy-start.5
  81.1 55.6 %shard_map.121 = bf16[1,512,512]{2,1,0:T(8,128)(2,1)S(1)} custom-call(f32[512,512]{1,0:T(8,128)S(1)} %bitcast.49), custom_call_target="tpu_custom_call" | custom-call | tf_op jit(solution)/shard_map/pallas_call | solution.py:273
  136.7 0.0 copy-done.7
  136.7 0.3 fusion.8
  137.1 0.3 convolution_bitcast_fusion.2
  137.4 0.0 copy-done.5
  137.4 0.3 fusion.1
  137.8 1.4 collective-permute-start
  139.2 0.3 convolution_bitcast_fusion.1
  139.5 0.2 pad_maximum_fusion
  139.7 2.9 %copy.17 = f32[512,2,512]{2,1,0:T(2,128)} copy(f32[512,2,512]{2,0,1:T(8,128)S(1)} %pad_maximum_fusion) | data formatting | bytes 4194304
  142.6 0.0 copy-start.8
  142.6 3.8 %collective-permute-done = bf16[256,512]{1,0:T(8,128)(2,1)S(1)} collective-permute-done((bf16[256,512]{1,0:T(8,128)(2,1)S(1)}, bf16[256,512]{1,0:T(8,128)(2,1)S(1)}, u32[]{:S(2)}, u32[]{:S(2)}) %collective-permute-start) | collective-permute-done | bytes 262176 | tf_op jit(solution)/shard_map/ppermute | solution.py:307
  146.5 0.7 fusion.17
  147.2 0.3 fusion.4
  147.4 0.0 copy-done.8
  147.5 0.5 convolution_bitcast_fusion
  147.9 0.3 fusion.2
  148.2 30.1 %shard_map.122 = bf16[2,512,256]{2,1,0:T(8,128)(2,1)S(1)} custom-call(f32[512,256]{1,0:T(8,128)S(1)} %pad_maximum_fusion.2.x_ref), custom_call_target="tpu_custom_call" | custom-call | tf_op jit(solution)/shard_map/pallas_call | solution.py:273
  178.3 0.7 slice_bitcast_fusion.3
  179.0 1.8 copy.18
  180.8 2.0 %maximum_convert_fusion = f32[256,1024]{1,0:T(8,128)} fusion(bf16[256,256]{1,0:T(8,128)(2,1)S(1)} %get-tuple-element.24, bf16[256,256]{1,0:T(8,128)(2,1)S(1)} %get-tuple-element.25, bf16[256,256]{1,0:T(8,128)(2,1)} %get-tuple-element.26, bf16[256,256]{1,0:T(8,128)(2,1)S(1)} %get-tuple-element.23), kind=kLoop, calls=%fused_computation.10 | loop fusion | flops 2097152 | bytes 1572864 | tf_op jit(solution)/shard_map/convert_element_type | solution.py:327
  (1 shorter events, 0.0 us)
Async XLA Ops:
  7.2 1.9 %copy-start = (bf16[1024,512]{1,0:T(8,128)(2,1)S(1)}, bf16[1024,512]{1,0:T(8,128)(2,1)}, u32[]{:S(2)}) copy-start(bf16[1024,512]{1,0:T(8,128)(2,1)} %param.9) | copy-start | bytes 3145732
  7.2 3.4 %copy-start.3 = (bf16[512,2,512]{2,1,0:T(2,128)(2,1)S(1)}, bf16[512,2,512]{2,1,0:T(2,128)(2,1)}, u32[]{:S(2)}) copy-start(bf16[512,2,512]{2,1,0:T(2,128)(2,1)} %param.11) | copy-start | bytes 3145732
  7.2 60.5 %all-gather.2.cloned.1.call-start = ((), (), s32[]{:S(2)}) async-start(), calls=%async_computation | async-start | bytes 4456448 | tf_op jit(solution)/shard_map/all_gather | solution.py:293
  12.1 1.0 copy-start.4
  12.1 1.3 copy-start.6
  13.4 54.2 %copy-start.1 = (bf16[128,4096]{1,0:T(8,128)(2,1)S(1)}, bf16[128,4096]{1,0:T(8,128)(2,1)}, u32[]{:S(2)}) copy-start(bf16[128,4096]{1,0:T(8,128)(2,1)} %q_ref.1) | copy-start | bytes 3145732
  67.7 1.2 copy-start.2
  68.9 67.8 %copy-start.7 = (bf16[512,1,512]{2,1,0:T(2,128)(2,1)S(1)}, bf16[512,1,512]{2,1,0:T(2,128)(2,1)}, u32[]{:S(2)}) copy-start(bf16[512,1,512]{2,1,0:T(2,128)(2,1)} %copy-done.6) | copy-start | bytes 1572868
  81.1 56.3 %copy-start.5 = (bf16[512,1,512]{2,1,0:T(2,128)(2,1)S(1)}, bf16[512,1,512]{2,1,0:T(2,128)(2,1)}, u32[]{:S(2)}) copy-start(bf16[512,1,512]{2,1,0:T(2,128)(2,1)} %copy-done.4) | copy-start | bytes 1572868
  137.8 8.7 %collective-permute-start = (bf16[256,512]{1,0:T(8,128)(2,1)S(1)}, bf16[256,512]{1,0:T(8,128)(2,1)S(1)}, u32[]{:S(2)}, u32[]{:S(2)}) collective-permute-start(bf16[256,512]{1,0:T(8,128)(2,1)S(1)} %fusion.1), channel_id=1, source_target_pairs={{0,1},{1,0},{2,3},{3,2},{4,5},{5,4},{6,7},{7,6},{8,9},{9,8},{10,11... | collective-permute-start | bytes 786440 | tf_op jit(solution)/shard_map/ppermute | solution.py:307
  142.6 4.8 %copy-start.8 = (bf16[256,1024]{1,0:T(8,128)(2,1)S(1)}, bf16[256,1024]{1,0:T(8,128)(2,1)}, u32[]{:S(2)}) copy-start(bf16[256,1024]{1,0:T(8,128)(2,1)} %param.8) | copy-start | bytes 1572868
Sparse Core Ops, SparseCore 0:
  10.8 56.8 all-gather.1

commit v4 on v3

--- a/solution.py
+++ b/solution.py
@@ -131,7 +131,7 @@
     group = QH // KVH
     per_tile = math.gcd(group, HEADS_PER_TILE)
     tiles = group // per_tile
-    block = 2 * tok if total % (2 * tok) == 0 else tok
+    block = next(n * tok for n in (4, 2, 1) if total % (n * tok) == 0)
     rows = per_tile * tok
     prefix_len = prefix_kv.shape[0] // 2
     row_block = pl.BlockSpec((tok, per_tile * HD), lambda g, j, pos: (0, g * tiles + j))

time: 190 us -> 182 us (0.958)
  Pallas kernels: 137 us -> 129 us
    pallas_call x3, Pallas kernels: 125 us -> 115 us  [all_sum(): pl.pallas_call(functools.partial(sum_kernel, levels, orders, paired), out...]
  transfers between devices with their start and end apart: 2 -> 2, of which waited for: 2 -> 2; matrix products, arithmetic and copies ran while one was open for 4% -> 4% of each run, Pallas kernels for 21% -> 22%
where the time goes in v4:
time: 182 us
  Pallas kernels  129 us (71%)
  waiting for transfers between devices  18.6 us (10%)
  between operations  14.2 us (8%)
  local copies, waits for them, and re-layouts  8.88 us (5%)
  other arithmetic  4.88 us (3%)
  matrix products  4.4 us (2%)
    pallas_call x3, Pallas kernels, all_sum(): pl.pallas_call(functools.partial(sum_kernel, levels, orders, paired), out...  115 us
    all_gather x1, waiting for transfers between devices, on_device(): lax.all_gather(jnp.concatenate([keys, values], 1), 'seq', axis=0, tiled=T...  14.9 us
    pallas_call x1, Pallas kernels, attention(): pl.pallas_call(attention_kernel, out_shape=(jax.ShapeDtypeStruct(queries....  14.1 us
    unnamed x20, local copies, waits for them, and re-layouts  6.68 us
    ppermute x1, waiting for transfers between devices, on_device(): theirs = lax.ppermute(mine, 'head', [(0, 1), (1, 0)])  3.72 us
  transfers between devices with their start and end apart: 2, of which 2 were waited for; matrix products, arithmetic and copies ran while one was open for 4% of the time, Pallas kernels for 22%

profile of v4, /device:TPU:0, one launch (start us, length us, event | category | flops | bytes accessed | tf_op | source)
XLA Modules:
  0.0 181.6 jit_solution(7840056266760113264)
XLA Ops:
  7.2 0.0 copy-start
  7.2 0.0 copy-start.3
  7.2 0.0 all-gather.2.cloned.1.call-start
  7.2 1.8 %pad_maximum_fusion.3 = bf16[128,1024]{1,0:T(8,128)(2,1)} fusion(bf16[128,512]{1,0:T(8,128)(2,1)} %param.14, bf16[128,512]{1,0:T(8,128)(2,1)} %param.13), kind=kLoop, calls=%fused_computation.18 | loop fusion | flops 524288 | bytes 524288 | tf_op jit(solution)/shard_map/concatenate | solution.py:293
  9.1 0.0 all-gather.2.cloned.1.call-update
  9.1 0.0 copy-done
  9.1 1.5 fusion.22
  10.6 0.0 copy-done.3
  10.6 1.5 fusion.21
  12.1 0.0 copy-start.4
  12.1 0.0 copy-start.6
  12.2 0.3 fusion.15
  12.5 0.3 fusion.16
  12.8 0.3 copy-done.4
  13.1 0.3 copy-done.6
  13.4 0.0 copy-start.1
  13.4 0.1 pad_maximum_fusion.1.x_ref
  13.5 39.2 %shard_map.119 = bf16[1,512,512]{2,1,0:T(8,128)(2,1)S(1)} custom-call(f32[512,512]{1,0:T(8,128)S(1)} %pad_maximum_fusion.1.x_ref), custom_call_target="tpu_custom_call" | custom-call | tf_op jit(solution)/shard_map/pallas_call | solution.py:273
  52.8 14.9 %all-gather.2.cloned.1.call-done.k_ref.v_ref = bf16[2048,1024]{1,0:T(8,128)(2,1)} async-done(((bf16[128,1024]{1,0:T(8,128)(2,1)}), bf16[2048,1024]{1,0:T(8,128)(2,1)}) %all-gather.2.cloned.1.call-update) | async-done | bytes 4194320 | tf_op jit(solution)/shard_map/all_gather | solution.py:293
  67.7 0.0 copy-done.1
  67.7 0.0 copy-start.2
  67.7 1.2 copy-done.2
  68.9 0.0 copy-start.7
  68.9 14.1 %shard_map.120 = (bf16[128,4096]{1,0:T(8,128)(2,1)}, f32[2,256,512]{2,1,0:T(8,128)S(1)}) custom-call(s32[1]{0:T(128)} %bitcast.pos_ref, bf16[128,4096]{1,0:T(8,128)(2,1)S(1)} %copy-done.1, bf16[128,4096]{1,0:T(8,128)(2,1)S(1)} %copy-done.2, bf16[2048,1024]{1,0:T(8,128)(2,1)} %all-gather.2.cloned.1.call-done.k_ref.v_ref, ...), custom_call_target="tpu_custom_call" | custom-call | tf_op jit(solution)/shard_map/pallas_call | solution.py:144
  83.0 0.0 copy-start.5
  83.0 44.9 %shard_map.121 = bf16[1,512,512]{2,1,0:T(8,128)(2,1)S(1)} custom-call(f32[512,512]{1,0:T(8,128)S(1)} %bitcast.49), custom_call_target="tpu_custom_call" | custom-call | tf_op jit(solution)/shard_map/pallas_call | solution.py:273
  127.9 0.0 copy-done.7
  127.9 0.3 fusion.8
  128.2 0.3 convolution_bitcast_fusion.2
  128.6 0.0 copy-done.5
  128.6 0.3 fusion.1
  128.9 1.5 collective-permute-start
  130.4 0.3 convolution_bitcast_fusion.1
  130.8 0.2 pad_maximum_fusion
  131.0 2.9 %copy.17 = f32[512,2,512]{2,1,0:T(2,128)} copy(f32[512,2,512]{2,0,1:T(8,128)S(1)} %pad_maximum_fusion) | data formatting | bytes 4194304
  133.9 0.0 copy-start.8
  133.9 3.7 %collective-permute-done = bf16[256,512]{1,0:T(8,128)(2,1)S(1)} collective-permute-done((bf16[256,512]{1,0:T(8,128)(2,1)S(1)}, bf16[256,512]{1,0:T(8,128)(2,1)S(1)}, u32[]{:S(2)}, u32[]{:S(2)}) %collective-permute-start) | collective-permute-done | bytes 262176 | tf_op jit(solution)/shard_map/ppermute | solution.py:307
  137.6 0.7 fusion.17
  138.4 0.3 fusion.4
  138.6 0.0 copy-done.8
  138.6 0.5 convolution_bitcast_fusion
  139.1 0.3 fusion.2
  139.4 30.8 %shard_map.122 = bf16[2,512,256]{2,1,0:T(8,128)(2,1)S(1)} custom-call(f32[512,256]{1,0:T(8,128)S(1)} %pad_maximum_fusion.2.x_ref), custom_call_target="tpu_custom_call" | custom-call | tf_op jit(solution)/shard_map/pallas_call | solution.py:273
  170.2 0.7 slice_bitcast_fusion.3
  170.9 1.8 copy.18
  172.7 2.0 %maximum_convert_fusion = f32[256,1024]{1,0:T(8,128)} fusion(bf16[256,256]{1,0:T(8,128)(2,1)S(1)} %get-tuple-element.24, bf16[256,256]{1,0:T(8,128)(2,1)S(1)} %get-tuple-element.25, bf16[256,256]{1,0:T(8,128)(2,1)} %get-tuple-element.26, bf16[256,256]{1,0:T(8,128)(2,1)S(1)} %get-tuple-element.23), kind=kLoop, calls=%fused_computation.10 | loop fusion | flops 2097152 | bytes 1572864 | tf_op jit(solution)/shard_map/convert_element_type | solution.py:327
  (1 shorter events, 0.0 us)
Async XLA Ops:
  7.2 1.9 %copy-start = (bf16[1024,512]{1,0:T(8,128)(2,1)S(1)}, bf16[1024,512]{1,0:T(8,128)(2,1)}, u32[]{:S(2)}) copy-start(bf16[1024,512]{1,0:T(8,128)(2,1)} %param.9) | copy-start | bytes 3145732
  7.2 3.4 %copy-start.3 = (bf16[512,2,512]{2,1,0:T(2,128)(2,1)S(1)}, bf16[512,2,512]{2,1,0:T(2,128)(2,1)}, u32[]{:S(2)}) copy-start(bf16[512,2,512]{2,1,0:T(2,128)(2,1)} %param.11) | copy-start | bytes 3145732
  7.2 60.5 %all-gather.2.cloned.1.call-start = ((), (), s32[]{:S(2)}) async-start(), calls=%async_computation | async-start | bytes 4456448 | tf_op jit(solution)/shard_map/all_gather | solution.py:293
  12.1 1.0 copy-start.4
  12.1 1.3 copy-start.6
  13.4 54.2 %copy-start.1 = (bf16[128,4096]{1,0:T(8,128)(2,1)S(1)}, bf16[128,4096]{1,0:T(8,128)(2,1)}, u32[]{:S(2)}) copy-start(bf16[128,4096]{1,0:T(8,128)(2,1)} %q_ref.1) | copy-start | bytes 3145732
  67.7 1.2 copy-start.2
  68.9 59.0 %copy-start.7 = (bf16[512,1,512]{2,1,0:T(2,128)(2,1)S(1)}, bf16[512,1,512]{2,1,0:T(2,128)(2,1)}, u32[]{:S(2)}) copy-start(bf16[512,1,512]{2,1,0:T(2,128)(2,1)} %copy-done.6) | copy-start | bytes 1572868
  83.0 45.6 %copy-start.5 = (bf16[512,1,512]{2,1,0:T(2,128)(2,1)S(1)}, bf16[512,1,512]{2,1,0:T(2,128)(2,1)}, u32[]{:S(2)}) copy-start(bf16[512,1,512]{2,1,0:T(2,128)(2,1)} %copy-done.4) | copy-start | bytes 1572868
  128.9 8.7 %collective-permute-start = (bf16[256,512]{1,0:T(8,128)(2,1)S(1)}, bf16[256,512]{1,0:T(8,128)(2,1)S(1)}, u32[]{:S(2)}, u32[]{:S(2)}) collective-permute-start(bf16[256,512]{1,0:T(8,128)(2,1)S(1)} %fusion.1), channel_id=1, source_target_pairs={{0,1},{1,0},{2,3},{3,2},{4,5},{5,4},{6,7},{7,6},{8,9},{9,8},{10,11... | collective-permute-start | bytes 786440 | tf_op jit(solution)/shard_map/ppermute | solution.py:307
  133.9 4.7 %copy-start.8 = (bf16[256,1024]{1,0:T(8,128)(2,1)S(1)}, bf16[256,1024]{1,0:T(8,128)(2,1)}, u32[]{:S(2)}) copy-start(bf16[256,1024]{1,0:T(8,128)(2,1)} %param.8) | copy-start | bytes 1572868
Sparse Core Ops, SparseCore 0:
  10.8 56.8 all-gather.1
